TPU v7x, 128 devices: a whole 4x4x4 slice. The times are simulated.
128 devices in a mesh: row: 8 (over x_lo, y), col: 16 (over x_hi, z, core).
Axes of the slice: x: 4 (x_hi: 2, x_lo: 2; x = x_hi * 2 + x_lo), y: 4, z: 4, core: 2. Of those that a mesh axis runs over, the one named last changes fastest.
Arguments:
- inverse: bfloat16 [26624, 26624], P('row', 'col'), may hold values from -6 to 6
- panels: bfloat16 [2, 8192, 512], P(None, 'col'), may hold values from -0.0625 to 0.0625
- block_slot: int32 [208], replicated, may hold values from 0 to 207, as said below
- list_ids: int32 [2, 64], replicated, may hold values from 0 to 207, as said below
Outputs:
- packed_panels: float32 [2, 16384, 512], P(None, ('row', 'col'))
- diag_update: float32 [2, 512, 512], replicated
Inputs may be any that keep to these rules, and one draw needn't show every extreme that they name: block_slot is a permutation of the slots. `list_ids`: each supernode lists distinct blocks; at most 16 of a supernode's listed blocks have slots in one grid row (slot // 26 equal), and in every supernode some grid row holds exactly 16. `list_ids`: in each aligned group of 4 list positions of a supernode, at most 1 listed blocks have slots in one grid column (slot // 13 equal).
All inputs are finite; a program needn't handle non-finite values.
Results may differ from a plain program's by a relative error of at most 0.0003.
Values may be sent and summed in bfloat16 or wider, within the bound.
A program may use at most 128 MiB of HBM per device.

v0:
```python
import jax
import jax.numpy as jnp
from jax import lax
from jax.sharding import PartitionSpec as P

BS = 128


def split_up(array, dim, devices):
    dims = array.shape
    pieces = array.reshape(*dims[:dim], devices, dims[dim] // devices, *dims[dim + 1 :])
    return jnp.moveaxis(pieces, dim, 0)


def sent_and_summed(array, axis, dim):
    pieces = split_up(array, dim, lax.axis_size(axis))
    arrived = lax.all_to_all(pieces, axis, split_axis=0, concat_axis=0, tiled=True)
    return arrived.astype(jnp.float32).sum(axis=0)


def lookup_slots(block_slot, list_ids):
    block_ids = jnp.arange(block_slot.shape[0], dtype=jnp.int32)
    matches = list_ids[..., None] == block_ids
    return jnp.sum(jnp.where(matches, block_slot, 0), axis=-1)


def exact_product(left_rows, right_rows):
    return jnp.dot(left_rows.astype(jnp.float32).T, right_rows, precision=lax.Precision.HIGHEST)


def local(inverse, panels, block_slot, list_ids):
    panel_width = panels.shape[2]
    row_blocks = inverse.shape[0] // BS
    col_blocks = inverse.shape[1] // BS
    listed = list_ids.shape[1]
    grid_rows = lax.axis_size("row")
    grid_cols = lax.axis_size("col")
    max_rows = 2 * listed // grid_rows
    own_rows = max_rows * BS // grid_cols
    shard_len = panels.shape[1] // BS
    slot_cap = (col_blocks + grid_cols - 1) // grid_cols
    my_row = lax.axis_index("row")
    my_col = lax.axis_index("col")
    slots = lookup_slots(block_slot, list_ids)
    grid_row = slots // row_blocks
    local_row = slots % row_blocks
    grid_col = slots // col_blocks
    local_col = slots % col_blocks
    a_blocks = inverse.reshape(row_blocks, BS, col_blocks * BS)
    positions = jnp.arange(listed, dtype=jnp.int32)
    col_ids = jnp.arange(col_blocks, dtype=jnp.int32)
    shard_of = positions // shard_len
    local_pos = my_col * shard_len + jnp.arange(shard_len, dtype=jnp.int32)
    panel_sums = []
    diag_terms = []
    for supernode in range(panels.shape[0]):
        cols_here = grid_col[supernode]
        in_row = grid_row[supernode] == my_row
        chosen_pos = jnp.argsort(jnp.where(in_row, positions, listed + positions), stable=True)[
            :max_rows
        ]
        is_valid = in_row[chosen_pos]
        picked = a_blocks[local_row[supernode][chosen_pos]]
        picked = jnp.where(is_valid[:, None, None], picked, jnp.zeros((), jnp.bfloat16)).reshape(
            max_rows * BS, col_blocks * BS
        )
        local_blocks = panels[supernode].reshape(shard_len, BS, panel_width)
        same_group = (
            (cols_here[:, None] == cols_here[None, :])
            & (shard_of[:, None] == shard_of[None, :])
            & (positions[None, :] < positions[:, None])
        )
        same_rank = jnp.sum(same_group.astype(jnp.int32), axis=1)
        dest_ids = jnp.arange(grid_cols * slot_cap, dtype=jnp.int32)
        send_pick = (
            (cols_here[local_pos] * slot_cap + same_rank[local_pos])[None, :] == dest_ids[:, None]
        ).astype(jnp.bfloat16)
        outgoing = jnp.einsum(
            "mj,jbw->mbw", send_pick, local_blocks, preferred_element_type=jnp.float32
        )
        outgoing = outgoing.astype(jnp.bfloat16).reshape(grid_cols * slot_cap * BS, panel_width)
        incoming = lax.all_to_all(outgoing, "col", split_axis=0, concat_axis=0, tiled=True)
        incoming = incoming.reshape(grid_cols * slot_cap, BS, panel_width)
        mine_here = cols_here == my_col
        to_column = (
            mine_here[:, None] & (local_col[supernode][:, None] == col_ids[None, :])
        ).astype(jnp.float32)
        to_slot = ((shard_of * slot_cap + same_rank)[:, None] == dest_ids[None, :]).astype(
            jnp.float32
        )
        select = jnp.dot(to_column.T, to_slot).astype(jnp.bfloat16)
        chosen = jnp.einsum("kj,jbw->kbw", select, incoming, preferred_element_type=jnp.float32)
        chosen = chosen.astype(jnp.bfloat16).reshape(col_blocks * BS, panel_width)
        place = ((chosen_pos[:, None] == local_pos[None, :]) & is_valid[:, None]).astype(
            jnp.bfloat16
        )
        left_local = jnp.einsum(
            "kj,jbw->kbw", place, local_blocks, preferred_element_type=jnp.float32
        )
        left_local = left_local.reshape(max_rows * BS, panel_width)

        def partial_rows(first_row, row_count, picked=picked, chosen=chosen):
            return jnp.dot(picked, chosen, preferred_element_type=jnp.float32)

        mine_sums = lax.psum_scatter(
            partial_rows(jnp.int32(0), own_rows * lax.axis_size("col")),
            "col",
            scatter_dimension=0,
            tiled=True,
        )
        own_left = sent_and_summed(left_local.astype(jnp.bfloat16), "col", 0).astype(jnp.bfloat16)
        contrib = exact_product(own_left, mine_sums)
        panel_sums.append(mine_sums)
        diag_terms.append(contrib)
    diag_total = lax.psum(jnp.stack(diag_terms), ("row", "col"))
    return (jnp.stack(panel_sums), -diag_total)


def solution(mesh):
    return jax.shard_map(
        local,
        mesh=mesh,
        in_specs=(P("row", "col"), P(None, "col", None), P(), P()),
        out_specs=(P(None, ("row", "col"), None), P()),
        check_vma=False,
    )
```

profile of v0, /device:TPU:1, one launch (start us, length us, event | category | flops | bytes accessed | tf_op | source)
XLA Modules:
  0.0 414.8 jit_solution(4478664436259446148)
XLA Ops:
  7.2 0.9 select_reduce_fusion
  8.1 1.3 fusion.60
  9.4 0.6 gather_fusion.8
  10.2 0.6 gather_fusion.9
  10.9 0.9 convolution_convert_fusion.2
  11.7 2.5 copy.41
  14.2 9.3 %all-to-all-start.1 = ((bf16[16,128,512]{2,1,0:T(8,128)(2,1)}), bf16[16,128,512]{2,1,0:T(8,128)(2,1)S(1)}, u32[]{:S(2)}, u32[]{:S(2)}) async-start(bf16[16,128,512]{2,1,0:T(8,128)(2,1)} %copy.41), calls=%async_computation.2 | async-start | bytes 4194304 | tf_op jit(solution)/shard_map/all_to_all | solution.py:82
  23.6 2.0 sort.32
  25.6 0.7 gather_fusion.6
  26.3 0.7 gather_fusion.5
  27.0 8.2 %gather_fusion.7 = bf16[16,128,1664]{2,1,0:T(8,128)(2,1)} fusion(bf16[26,128,1664]{2,1,0:T(8,128)(2,1)} %bitcast.73, s32[1024]{0:T(1024)S(1)} %pad_clamp_fusion), kind=kCustom, calls=%fused_computation.7 | custom fusion | bytes 13631552 | tf_op jit(solution)/shard_map/gather | solution.py:63
  35.2 6.4 %broadcast_select_fusion = bf16[16,128,1664]{2,1,0:T(8,128)(2,1)} fusion(bf16[16,128,1664]{2,1,0:T(8,128)(2,1)} %gather_fusion.7, pred[16]{0:T(512)(128)(4,1)S(1)} %gather_fusion.5), kind=kLoop, calls=%fused_computation.10 | loop fusion | flops 3407872 | bytes 13631504 | tf_op jit(solution)/shard_map/jit(_where)/select_n | solution.py:64
  41.6 10.4 %all-to-all-done.1 = bf16[16,128,512]{2,1,0:T(8,128)(2,1)S(1)} async-done(((bf16[16,128,512]{2,1,0:T(8,128)(2,1)}), bf16[16,128,512]{2,1,0:T(8,128)(2,1)S(1)}, u32[]{:S(2)}, u32[]{:S(2)}) %all-to-all-start.1) | async-done | bytes 2097184 | tf_op jit(solution)/shard_map/all_to_all | solution.py:82
  52.0 2.8 fusion.7
  54.8 2.6 copy.43
  57.4 8.6 %fusion.64 = f32[2048,512]{1,0:T(8,128)} fusion(bf16[2048,1664]{1,0:T(8,128)(2,1)} %bitcast.76, bf16[1664,512]{1,0:T(8,128)(2,1)S(1)} %bitcast.81), kind=kOutput, calls=%fused_computation.117 | convolution fusion | flops 3489660928 | bytes 12713984 | tf_op jit(solution)/shard_map/dot_general | solution.py:103
  66.0 0.6 gather_fusion.3
  66.7 0.6 gather_fusion.4
  67.3 0.9 convolution_convert_fusion.3
  68.2 2.5 copy.37
  70.7 7.1 %all-to-all-start = ((bf16[16,128,512]{2,1,0:T(8,128)(2,1)}), bf16[16,128,512]{2,1,0:T(8,128)(2,1)S(1)}, u32[]{:S(2)}, u32[]{:S(2)}) async-start(bf16[16,128,512]{2,1,0:T(8,128)(2,1)} %copy.37), calls=%async_computation | async-start | bytes 4194304 | tf_op jit(solution)/shard_map/all_to_all | solution.py:82
  78.0 2.0 sort.31
  80.1 0.7 gather_fusion.1
  80.8 8.8 %gather_fusion.2 = bf16[16,128,1664]{2,1,0:T(8,128)(2,1)} fusion(bf16[26,128,1664]{2,1,0:T(8,128)(2,1)} %bitcast.74, s32[1024]{0:T(1024)S(1)} %pad_clamp_fusion.3), kind=kCustom, calls=%fused_computation.2 | custom fusion | bytes 13631552 | tf_op jit(solution)/shard_map/gather | solution.py:63
  89.5 0.7 gather_fusion
  90.2 6.4 %broadcast_select_fusion.1 = bf16[16,128,1664]{2,1,0:T(8,128)(2,1)} fusion(bf16[16,128,1664]{2,1,0:T(8,128)(2,1)} %gather_fusion.2, pred[16]{0:T(512)(128)(4,1)S(1)} %gather_fusion), kind=kLoop, calls=%fused_computation.11 | loop fusion | flops 3407872 | bytes 13631504 | tf_op jit(solution)/shard_map/jit(_where)/select_n | solution.py:64
  96.6 9.7 %all-to-all-done = bf16[16,128,512]{2,1,0:T(8,128)(2,1)S(1)} async-done(((bf16[16,128,512]{2,1,0:T(8,128)(2,1)}), bf16[16,128,512]{2,1,0:T(8,128)(2,1)S(1)}, u32[]{:S(2)}, u32[]{:S(2)}) %all-to-all-start) | async-done | bytes 2097184 | tf_op jit(solution)/shard_map/all_to_all | solution.py:82
  106.3 2.8 fusion.4
  109.1 2.6 copy.39
  111.7 8.5 %fusion.63 = f32[2048,512]{1,0:T(8,128)} fusion(bf16[2048,1664]{1,0:T(8,128)(2,1)} %bitcast.75, bf16[1664,512]{1,0:T(8,128)(2,1)S(1)} %bitcast.82), kind=kOutput, calls=%fused_computation.116 | convolution fusion | flops 3489660928 | bytes 12713984 | tf_op jit(solution)/shard_map/dot_general | solution.py:103
  120.3 0.9 convolution_convert_fusion
  121.2 2.5 copy.47
  123.7 10.4 %all-to-all-start.3 = ((bf16[16,128,512]{2,1,0:T(8,128)(2,1)}), bf16[16,128,512]{2,1,0:T(8,128)(2,1)S(1)}, u32[]{:S(2)}, u32[]{:S(2)}) async-start(bf16[16,128,512]{2,1,0:T(8,128)(2,1)} %copy.47), calls=%async_computation.5 | async-start | bytes 4194304 | tf_op jit(solution)/shard_map/all_to_all | solution.py:17
  134.0 0.9 convolution_convert_fusion.1
  134.9 2.5 copy.45
  137.3 28.3 %all-to-all-done.3 = bf16[16,128,512]{2,1,0:T(8,128)(2,1)S(1)} async-done(((bf16[16,128,512]{2,1,0:T(8,128)(2,1)}), bf16[16,128,512]{2,1,0:T(8,128)(2,1)S(1)}, u32[]{:S(2)}, u32[]{:S(2)}) %all-to-all-start.3) | async-done | bytes 2097184 | tf_op jit(solution)/shard_map/all_to_all | solution.py:17
  165.7 7.6 %all-to-all-start.2 = ((bf16[16,128,512]{2,1,0:T(8,128)(2,1)}), bf16[16,128,512]{2,1,0:T(8,128)(2,1)}, u32[]{:S(2)}, u32[]{:S(2)}) async-start(bf16[16,128,512]{2,1,0:T(8,128)(2,1)} %copy.45), calls=%async_computation.4 | async-start | bytes 4194304 | tf_op jit(solution)/shard_map/all_to_all | solution.py:17
  173.5 0.3 reduce_sum.55
  173.8 28.0 %all-to-all-done.2 = bf16[16,128,512]{2,1,0:T(8,128)(2,1)} async-done(((bf16[16,128,512]{2,1,0:T(8,128)(2,1)}), bf16[16,128,512]{2,1,0:T(8,128)(2,1)}, u32[]{:S(2)}, u32[]{:S(2)}) %all-to-all-start.2) | async-done | bytes 2097184 | tf_op jit(solution)/shard_map/all_to_all | solution.py:17
  201.8 1.9 reduce_sum.54
  203.8 1.6 convolution_bitcast_fusion
  205.4 43.9 %reduce-scatter.3.cloned.1.call-done = f32[128,512]{1,0:T(8,128)} async-done(((f32[2048,512]{1,0:T(8,128)}), f32[128,512]{1,0:T(8,128)}) %reduce-scatter.3.cloned.1.call-update) | async-done | bytes 262160 | tf_op jit(solution)/shard_map/reduce_scatter | solution.py:105
  249.2 1.6 convolution_bitcast_fusion.1
  250.8 1.5 pad_maximum_fusion
  252.4 0.9 copy-done
  253.4 0.8 pad_maximum_fusion.1
  254.2 150.9 %all-reduce.2.cloned.1.call-done = f32[2,512,512]{2,1,0:T(8,128)} async-done(((f32[2,512,512]{2,1,0:T(8,128)}), f32[2,512,512]{2,1,0:T(8,128)}) %all-reduce.2.cloned.1.call-update) | async-done | bytes 2097168 | tf_op jit(solution)/shard_map/psum | solution.py:115
  405.1 3.1 neg.3
  (34 shorter events, 1.0 us)
Async XLA Ops:
  14.2 37.8 %all-to-all-start.1 = ((bf16[16,128,512]{2,1,0:T(8,128)(2,1)}), bf16[16,128,512]{2,1,0:T(8,128)(2,1)S(1)}, u32[]{:S(2)}, u32[]{:S(2)}) async-start(bf16[16,128,512]{2,1,0:T(8,128)(2,1)} %copy.41), calls=%async_computation.2 | async-start | bytes 4194304 | tf_op jit(solution)/shard_map/all_to_all | solution.py:82
  23.5 180.2 %reduce-scatter.5.cloned.1.call-start = ((), (), s32[]{:S(2)}) async-start(), calls=%async_computation.7 | async-start | bytes 4456448 | tf_op jit(solution)/shard_map/reduce_scatter | solution.py:105
  70.7 35.6 %all-to-all-start = ((bf16[16,128,512]{2,1,0:T(8,128)(2,1)}), bf16[16,128,512]{2,1,0:T(8,128)(2,1)S(1)}, u32[]{:S(2)}, u32[]{:S(2)}) async-start(bf16[16,128,512]{2,1,0:T(8,128)(2,1)} %copy.37), calls=%async_computation | async-start | bytes 4194304 | tf_op jit(solution)/shard_map/all_to_all | solution.py:82
  77.8 171.4 %reduce-scatter.3.cloned.1.call-start = ((), (), s32[]{:S(2)}) async-start(), calls=%async_computation.6 | async-start | bytes 4456448 | tf_op jit(solution)/shard_map/reduce_scatter | solution.py:105
  123.7 42.0 %all-to-all-start.3 = ((bf16[16,128,512]{2,1,0:T(8,128)(2,1)}), bf16[16,128,512]{2,1,0:T(8,128)(2,1)S(1)}, u32[]{:S(2)}, u32[]{:S(2)}) async-start(bf16[16,128,512]{2,1,0:T(8,128)(2,1)} %copy.47), calls=%async_computation.5 | async-start | bytes 4194304 | tf_op jit(solution)/shard_map/all_to_all | solution.py:17
  165.7 36.2 %all-to-all-start.2 = ((bf16[16,128,512]{2,1,0:T(8,128)(2,1)}), bf16[16,128,512]{2,1,0:T(8,128)(2,1)}, u32[]{:S(2)}, u32[]{:S(2)}) async-start(bf16[16,128,512]{2,1,0:T(8,128)(2,1)} %copy.45), calls=%async_computation.4 | async-start | bytes 4194304 | tf_op jit(solution)/shard_map/all_to_all | solution.py:17
  173.3 231.9 %all-reduce.2.cloned.1.call-start = ((), (), s32[]{:S(2)}) async-start(), calls=%async_computation.8 | async-start | bytes 4194304 | tf_op jit(solution)/shard_map/psum | solution.py:115
  252.3 0.9 copy-start
  252.3 1.0 copy-start.1
Sparse Core Ops, SparseCore 0:
  66.1 95.6 reduce-scatter.4
  166.4 82.7 reduce-scatter.2
  254.6 150.4 all-reduce.1
where the time goes:
time: 416 us; the launch traced here: 415 us
  waiting for transfers between devices  271 us (65%)
  local copies, waits for them, and re-layouts  39.6 us (10%)
  starting transfers between devices  34.9 us (8%)
  matrix products  29.4 us (7%)
  other arithmetic  25.7 us (6%)
  between operations  13.9 us (3%)
    psum x1, waiting for transfers between devices, local(): diag_total = lax.psum(jnp.stack(diag_terms), ('row', 'col'))  151 us
    all_to_all x2, waiting for transfers between devices, sent_and_summed(): lax.all_to_all(pieces, axis, split_axis=0, concat_axis=0, tiled=True)  56.3 us
    reduce_scatter x2, waiting for transfers between devices, local(): lax.psum_scatter(partial_rows(jnp.int32(0), own_rows * lax.axis_size('col...  43.9 us
    all_to_all x2, waiting for transfers between devices, local(): lax.all_to_all(outgoing, 'col', split_axis=0, concat_axis=0, tiled=True)  20.1 us
    gather x4, local copies, waits for them, and re-layouts, local(): picked = a_blocks[local_row[supernode][chosen_pos]]  18.3 us
    all_to_all x2, starting transfers between devices, sent_and_summed(): lax.all_to_all(pieces, axis, split_axis=0, concat_axis=0, tiled=True)  18 us
    dot_general x2, matrix products, partial_rows(): return jnp.dot(picked, chosen, preferred_element_type=jnp.float32)  17.1 us
    all_to_all x2, starting transfers between devices, local(): lax.all_to_all(outgoing, 'col', split_axis=0, concat_axis=0, tiled=True)  16.4 us
  transfers between devices with their start and end apart: 7, of which 6 were waited for; matrix products, arithmetic and copies ran while one was open for 16% of the time, Pallas kernels for 0%

commit v1 on v0

v1 whole, which is shorter than its diff:
```python
import functools

import jax
import jax.numpy as jnp
from jax import lax
from jax.experimental import pallas as pl
from jax.experimental.pallas import tpu as pltpu
from jax.sharding import PartitionSpec as P

BS = 128
MESH = pl.DeviceIdType.MESH
F32 = jnp.float32
BF16 = jnp.bfloat16


def tables(block_slot, list_ids, n_rows, n_cols):
    n_blocks, listed = block_slot.shape[0], list_ids.shape[1]
    ids = jnp.arange(n_blocks, dtype=jnp.int32)
    slots = jnp.sum(jnp.where(list_ids[..., None] == ids, block_slot, 0), axis=-1)
    col_blocks, row_blocks = n_blocks // n_cols, n_blocks // n_rows
    col = slots // col_blocks
    row = slots // row_blocks
    pos = jnp.arange(listed, dtype=jnp.int32)
    before = pos[None, :] < pos[:, None]
    rank = jnp.sum(((col[:, :, None] == col[:, None, :]) & before).astype(jnp.int32), axis=-1)
    kth = jnp.sum(((row[:, :, None] == row[:, None, :]) & before).astype(jnp.int32), axis=-1)
    code = 1 + (slots * 16 + rank) * 64 + pos

    def listed_in(group, index, groups):
        to_group = group[:, None, None, :] == jnp.arange(groups, dtype=jnp.int32)[:, None, None]
        to_index = index[:, None, None, :] == jnp.arange(16, dtype=jnp.int32)[:, None]
        return jnp.sum(jnp.where(to_group & to_index, code[:, None, None, :], 0), axis=-1)

    by_col = listed_in(col, rank, n_cols)
    by_row = listed_in(row, kth, n_rows)
    col_code, row_code = jnp.maximum(by_col - 1, 0), jnp.maximum(by_row - 1, 0)
    shard = listed // n_cols
    col_table = jnp.stack([(by_col > 0).astype(jnp.int32), col_code % 64 // shard, col_code // 1024 % col_blocks])
    row_table = jnp.stack([(by_row > 0).astype(jnp.int32), row_code // 1024 % row_blocks])
    of_col = jnp.repeat(row_code, n_cols // n_rows, axis=1)
    here = jnp.repeat(by_row, n_cols // n_rows, axis=1) > 0
    here &= of_col // 1024 // col_blocks == jnp.arange(n_cols, dtype=jnp.int32)[:, None]
    left_table = jnp.stack([here.astype(jnp.int32), jnp.where(here, of_col // 64 % 16, 0)])
    return col, col_table, row_table, left_table


def kernel(
    n_rows, n_cols, x_his,
    inv_hbm, pan, cols, by_col, by_row, by_k,
    out, diag,
    a_all, a_pick, p_send, p_recv, ag_send, p_all, l_send, l_recv, m_send, left,
    part, core_recv, z_recv, x_recv, d_part, d_sib, d_row, d_row_in, d_col, d_col_in, e_piece, e_col, e_row,
    a_sem, p_ss, p_rs, ag_ss, ag_rs, l_ss, l_rs, m_ss, m_rs, c_ss, c_rs, z_ss, z_rs, x_ss, x_rs,
    ds_ss, ds_rs, dr_ss, dr_rs, dc_ss, dc_rs, ec_ss, ec_rs, er_ss, er_rs, es_ss, es_rs,
):
    supers = pan.shape[0]
    sub = BS // n_rows
    col_blocks = a_all.shape[0]
    shard = pan.shape[1] // BS
    width = pan.shape[2]
    chips = n_cols // 2
    zs = chips // x_his
    me_r, me_c = lax.axis_index("row"), lax.axis_index("col")
    core = lax.rem(me_c, 2)
    chip = me_c // 2
    x_hi, z = chip // zs, lax.rem(chip, zs)
    sibling = (me_r, me_c + 1 - 2 * core)

    def remote(src, dst, ss, rs, to):
        return pltpu.make_async_remote_copy(
            src_ref=src, dst_ref=dst, send_sem=ss, recv_sem=rs, device_id=to, device_id_type=MESH
        )

    def load_a(b):
        columns = pl.ds(pl.multiple_of(b * BS, BS), BS)
        return pltpu.make_async_copy(inv_hbm.at[:, :, columns], a_all.at[b], a_sem.at[b])

    @pl.loop(0, col_blocks)
    def _(b):
        load_a(b).start()

    barrier = pltpu.get_barrier_semaphore()

    @pl.loop(1, n_cols)
    def _(d):
        pl.semaphore_signal(barrier, inc=1, device_id=(me_r, lax.rem(me_c + d, n_cols)), device_id_type=MESH)

    @pl.loop(1, n_rows)
    def _(d):
        pl.semaphore_signal(barrier, inc=1, device_id=(lax.rem(me_r + d, n_rows), me_c), device_id_type=MESH)

    def pick_for(c, s):
        piece = jnp.zeros((sub, width), BF16)
        for q in range(shard):
            block = pan[s, pl.ds(pl.multiple_of(q * BS + me_r * sub, sub), sub), :]
            piece = jnp.where(cols[s, me_c * shard + q] == c, block, piece)
        return piece

    @pl.loop(1, n_cols)
    def _(d):
        for s in range(supers):
            p_send[d, s] = pick_for(lax.rem(me_c + d, n_cols), s)

    for s in range(supers):
        p_recv[me_c, s] = pick_for(me_c, s)

    pl.semaphore_wait(barrier, n_cols + n_rows - 2)

    def p_copy(d):
        return remote(p_send.at[d], p_recv.at[me_c], p_ss.at[d], p_rs.at[d], (me_r, lax.rem(me_c + d, n_cols)))

    def p_arrive(d):
        return remote(p_send.at[d], p_recv.at[lax.rem(me_c - d + n_cols, n_cols)], p_ss.at[d], p_rs.at[d], (me_r, lax.rem(me_c + d, n_cols)))

    @pl.loop(1, n_cols)
    def _(d):
        p_copy(d).start()

    @pl.loop(1, n_cols)
    def _(d):
        p_arrive(d).wait_recv()

    def ag_copy(s, d):
        return remote(ag_send.at[s], p_all.at[s, :, me_r], ag_ss.at[s, d], ag_rs.at[s, d], (lax.rem(me_r + d, n_rows), me_c))

    def ag_arrive(s, d):
        return remote(ag_send.at[s], p_all.at[s, :, lax.rem(me_r - d + n_rows, n_rows)], ag_ss.at[s, d], ag_rs.at[s, d], (lax.rem(me_r + d, n_rows), me_c))

    for s in range(supers):
        @pl.loop(0, col_blocks)
        def _(i, s=s):
            block = p_recv[by_col[1, s, me_c, i], s]
            block = jnp.where(by_col[0, s, me_c, i] == 1, block, jnp.zeros_like(block))
            ag_send[s, i] = block
            p_all[s, i, me_r] = block

        @pl.loop(1, n_rows)
        def _(d, s=s):
            ag_copy(s, d).start()

    def left_for(k, s):
        block = ag_send[s, by_k[1, s, me_c, k]]
        return jnp.where(by_k[0, s, me_c, k] == 1, block, jnp.zeros_like(block))

    def l_copy(d):
        return remote(l_send.at[d], l_recv.at[me_c], l_ss.at[d], l_rs.at[d], (me_r, lax.rem(me_c + d, n_cols)))

    def l_arrive(d):
        return remote(l_send.at[d], l_recv.at[lax.rem(me_c - d + n_cols, n_cols)], l_ss.at[d], l_rs.at[d], (me_r, lax.rem(me_c + d, n_cols)))

    for s in range(supers):
        l_recv[me_c, s] = left_for(me_c, s)

    @pl.loop(1, n_cols)
    def _(d):
        for s in range(supers):
            l_send[d, s] = left_for(lax.rem(me_c + d, n_cols), s)
        l_copy(d).start()

    def c_copy(s, h):
        return remote(part.at[s, 0, h], core_recv.at[s, h], c_ss.at[s, h], c_rs.at[s, h], sibling)

    def z_copy(s, h, d):
        to = (me_r, (x_hi * zs + lax.rem(z + d, zs)) * 2 + core)
        return remote(part.at[s, 1, h, lax.rem(z + d, zs)], z_recv.at[s, h, d], z_ss.at[s, h, d], z_rs.at[s, h, d], to)

    def products(s):
        @pl.loop(1, n_rows)
        def _(d):
            ag_arrive(s, d).wait_recv()

        if s == 0:
            @pl.loop(0, col_blocks)
            def _(b):
                load_a(b).wait()

        @pl.loop(0, 2 * x_his)
        def _(i):
            mine, h = i // x_his, lax.rem(i, x_his)
            for u in range(zs):
                k = 2 * (h * zs + u) + jnp.where(mine == 1, core, 1 - core)
                a_row = by_row[1, s, me_r, k]
                for b in range(col_blocks):
                    a_pick[u * BS : (u + 1) * BS, b * BS : (b + 1) * BS] = a_all[by_col[2, s, me_c, b], a_row]
            product = jnp.dot(a_pick[...], p_all[s].reshape(col_blocks * BS, width), preferred_element_type=F32)
            part[s, mine, h] = product.reshape(zs, BS, width)

            @pl.when(mine == 0)
            def _():
                c_copy(s, h).start()

        for h in range(x_his):
            c_copy(s, h).wait_recv()
            part[s, 1, h] = part[s, 1, h] + core_recv[s, h]
            for d in range(1, zs):
                z_copy(s, h, d).start()

    def m_copy(d):
        return remote(m_send.at[d], left.at[:, me_r], m_ss.at[d], m_rs.at[d], (lax.rem(me_r + d, n_rows), me_c))

    def m_arrive(d):
        return remote(m_send.at[d], left.at[:, lax.rem(me_r - d + n_rows, n_rows)], m_ss.at[d], m_rs.at[d], (lax.rem(me_r + d, n_rows), me_c))

    products(0)

    @pl.loop(1, n_cols)
    def _(d):
        l_arrive(d).wait_recv()

    left[:, me_r] = l_recv[2 * me_r] + l_recv[2 * me_r + 1]

    @pl.loop(1, n_rows)
    def _(d):
        g = lax.rem(me_r + d, n_rows)
        m_send[d] = l_recv[2 * g] + l_recv[2 * g + 1]
        m_copy(d).start()

    products(1)

    @pl.loop(1, n_rows)
    def _(d):
        m_arrive(d).wait_recv()

    def x_copy(s):
        to = (me_r, ((1 - x_hi) * zs + z) * 2 + core)
        return remote(part.at[s, 1, 1 - x_hi, z], x_recv.at[s], x_ss.at[s], x_rs.at[s], to)

    def over_z(s, h):
        total = part[s, 1, h, z]
        for d in range(1, zs):
            z_copy(s, h, d).wait_recv()
            total = total + z_recv[s, h, d]
        part[s, 1, h, z] = total

    half = width // 2
    piece = half // n_rows

    def ds_copy(s):
        there = pl.ds(pl.multiple_of((1 - core) * half, half), half)
        return remote(d_part.at[s, there], d_sib.at[s], ds_ss.at[s], ds_rs.at[s], sibling)

    def dr_copy(s, d):
        g = lax.rem(me_r + d, n_rows)
        return remote(d_row.at[s, g], d_row_in.at[s, d], dr_ss.at[s, d], dr_rs.at[s, d], (g, me_c))

    def chip_at(d):
        return lax.rem(chip + d, chips)

    def dc_copy(s, d):
        t = chip_at(d)
        return remote(d_col.at[s, t], d_col_in.at[s, d], dc_ss.at[s, d], dc_rs.at[s, d], (me_r, 2 * t + core))

    def ec_copy(s, d, source):
        return remote(e_piece.at[s], e_col.at[s, source], ec_ss.at[s, d], ec_rs.at[s, d], (me_r, 2 * chip_at(d) + core))

    def rows_of(r):
        return pl.ds(pl.multiple_of(core * half + r * piece, piece), piece)

    def er_copy(s, d, source):
        to = (lax.rem(me_r + d, n_rows), me_c)
        return remote(e_row.at[s], diag.at[s, rows_of(source)], er_ss.at[s, d], er_rs.at[s, d], to)

    def es_copy(s, half_of):
        there = pl.ds(pl.multiple_of(half_of * half, half), half)
        return remote(diag.at[s, there], diag.at[s, there], es_ss.at[s], es_rs.at[s], sibling)

    def finish_sums(s):
        x_copy(s).wait_recv()
        total = part[s, 1, x_hi, z] + x_recv[s]
        valid = by_row[0, s, me_r, me_c] == 1
        total = jnp.where(valid, total, jnp.zeros_like(total))
        out[s] = total
        high = total.astype(BF16)
        low = (total - high.astype(F32)).astype(BF16)
        block = left[s].reshape(BS, width)
        contract = functools.partial(
            lax.dot_general, dimension_numbers=(((0,), (0,)), ((), ())), preferred_element_type=F32
        )
        d_part[s] = -(contract(block, high) + contract(block, low))
        ds_copy(s).start()

    def over_cores(s):
        ds_copy(s).wait_recv()
        here = pl.ds(pl.multiple_of(core * half, half), half)
        total = d_part[s, here] + d_sib[s]
        d_row[s] = total.reshape(n_rows, piece, width)

        @pl.loop(1, n_rows)
        def _(d):
            dr_copy(s, d).start()

    def over_rows(s):
        total = d_row[s, me_r]
        for d in range(1, n_rows):
            dr_copy(s, d).wait_recv()
            total = total + d_row_in[s, d]
        for t in range(chips):
            d_col[s, t] = total[(t // 2) * 8 : (t // 2) * 8 + 8, (t % 2) * half : (t % 2) * half + half]

        @pl.loop(1, chips)
        def _(d):
            dc_copy(s, d).start()

    def over_chips(s):
        total = d_col[s, chip]
        for d in range(1, chips):
            dc_copy(s, d).wait_recv()
            total = total + d_col_in[s, d]
        e_piece[s] = total
        e_col[s, chip] = total

        @pl.loop(1, chips)
        def _(d):
            ec_copy(s, d, chip).start()

    def back_over_chips(s):
        @pl.loop(1, chips)
        def _(d):
            ec_copy(s, d, lax.rem(chip - d + chips, chips)).wait_recv()

        for t in range(chips):
            e_row[s, (t // 2) * 8 : (t // 2) * 8 + 8, (t % 2) * half : (t % 2) * half + half] = e_col[s, t]
        diag[s, rows_of(me_r)] = e_row[s]

        @pl.loop(1, n_rows)
        def _(d):
            er_copy(s, d, me_r).start()

    def back_over_rows(s):
        @pl.loop(1, n_rows)
        def _(d):
            er_copy(s, d, lax.rem(me_r - d + n_rows, n_rows)).wait_recv()

        es_copy(s, core).start()

    over_z(0, 1 - x_hi)
    x_copy(0).start()
    over_z(0, x_hi)
    finish_sums(0)
    over_cores(0)
    over_z(1, 1 - x_hi)
    x_copy(1).start()
    over_z(1, x_hi)
    over_rows(0)
    finish_sums(1)
    over_cores(1)
    over_chips(0)
    over_rows(1)
    back_over_chips(0)
    over_chips(1)
    back_over_rows(0)
    back_over_chips(1)
    back_over_rows(1)

    @pl.loop(1, n_cols)
    def _(d):
        p_copy(d).wait_send()
        l_copy(d).wait_send()

    @pl.loop(1, n_rows)
    def _(d):
        m_copy(d).wait_send()

    for s in range(supers):
        @pl.loop(1, n_rows)
        def _(d, s=s):
            ag_copy(s, d).wait_send()
            dr_copy(s, d).wait_send()
            er_copy(s, d, me_r).wait_send()

        @pl.loop(1, chips)
        def _(d, s=s):
            dc_copy(s, d).wait_send()
            ec_copy(s, d, chip).wait_send()

        for h in range(x_his):
            c_copy(s, h).wait_send()
            for d in range(1, zs):
                z_copy(s, h, d).wait_send()
        x_copy(s).wait_send()
        ds_copy(s).wait_send()
        es_copy(s, core).wait_send()
        es_copy(s, 1 - core).wait_recv()


def local(n_rows, n_cols, inverse, panels, block_slot, list_ids):
    supers, _, width = panels.shape
    col_blocks = inverse.shape[1] // BS
    sub = BS // n_rows
    x_his = 2
    chips = n_cols // 2
    zs = chips // x_his
    half = width // 2
    piece = half // n_rows
    lists = tables(block_slot, list_ids, n_rows, n_cols)
    blocks = inverse.reshape(-1, BS, inverse.shape[1])
    vmem = pl.BlockSpec(memory_space=pltpu.VMEM)
    smem = pl.BlockSpec(memory_space=pltpu.SMEM)
    dma = pltpu.SemaphoreType.DMA
    scratch = [
        pltpu.VMEM((col_blocks, blocks.shape[0], BS, BS), BF16),
        pltpu.VMEM((zs * BS, col_blocks * BS), BF16),
        pltpu.VMEM((n_cols, supers, sub, width), BF16),
        pltpu.VMEM((n_cols, supers, sub, width), BF16),
        pltpu.VMEM((supers, col_blocks, sub, width), BF16),
        pltpu.VMEM((supers, col_blocks, n_rows, sub, width), BF16),
        pltpu.VMEM((n_cols, supers, sub, width), BF16),
        pltpu.VMEM((n_cols, supers, sub, width), BF16),
        pltpu.VMEM((n_rows, supers, sub, width), BF16),
        pltpu.VMEM((supers, n_rows, sub, width), BF16),
        pltpu.VMEM((supers, 2, x_his, zs, BS, width), F32),
        pltpu.VMEM((supers, x_his, zs, BS, width), F32),
        pltpu.VMEM((supers, x_his, zs, BS, width), F32),
        pltpu.VMEM((supers, BS, width), F32),
        pltpu.VMEM((supers, width, width), F32),
        pltpu.VMEM((supers, half, width), F32),
        pltpu.VMEM((supers, n_rows, piece, width), F32),
        pltpu.VMEM((supers, n_rows, piece, width), F32),
        pltpu.VMEM((supers, chips, 8, half), F32),
        pltpu.VMEM((supers, chips, 8, half), F32),
        pltpu.VMEM((supers, 8, half), F32),
        pltpu.VMEM((supers, chips, 8, half), F32),
        pltpu.VMEM((supers, piece, width), F32),
        dma((col_blocks,)),
        dma((n_cols,)), dma((n_cols,)),
        dma((supers, n_rows)), dma((supers, n_rows)),
        dma((n_cols,)), dma((n_cols,)),
        dma((n_rows,)), dma((n_rows,)),
        dma((supers, x_his)), dma((supers, x_his)),
        dma((supers, x_his, zs)), dma((supers, x_his, zs)),
        dma((supers,)), dma((supers,)),
        dma((supers,)), dma((supers,)),
        dma((supers, n_rows)), dma((supers, n_rows)),
        dma((supers, chips)), dma((supers, chips)),
        dma((supers, chips)), dma((supers, chips)),
        dma((supers, n_rows)), dma((supers, n_rows)),
        dma((supers,)), dma((supers,)),
    ]
    return pl.pallas_call(
        functools.partial(kernel, n_rows, n_cols, x_his),
        out_shape=(
            jax.ShapeDtypeStruct((supers, BS, width), F32),
            jax.ShapeDtypeStruct((supers, width, width), F32),
        ),
        in_specs=[pl.BlockSpec(memory_space=pl.ANY), vmem, smem, smem, smem, smem],
        out_specs=(vmem, vmem),
        scratch_shapes=scratch,
        compiler_params=pltpu.CompilerParams(
            collective_id=0, has_side_effects=True, vmem_limit_bytes=60 * 2**20
        ),
    )(blocks, panels, *lists)


def solution(mesh):
    n_rows, n_cols = mesh.shape["row"], mesh.shape["col"]
    return jax.shard_map(
        functools.partial(local, n_rows, n_cols),
        mesh=mesh,
        in_specs=(P("row", "col"), P(None, "col", None), P(), P()),
        out_specs=(P(None, ("row", "col"), None), P()),
        check_vma=False,
    )
```

time: 416 us -> 159 us (0.38)
  waiting for transfers between devices: 271 us -> 0 us
  Pallas kernels: 0 us -> 148 us
  starting transfers between devices: 34.9 us -> 0 us
  local copies, waits for them, and re-layouts: 39.6 us -> 4.99 us
  matrix products: 29.4 us -> 0 us
  other arithmetic: 25.7 us -> 4.11 us
  between operations: 13.9 us -> 0.76 us
    psum x1 -> x0, waiting for transfers between devices: 151 us -> none  [local(): diag_total = lax.psum(jnp.stack(diag_terms), ('row', 'col'))]
    pallas_call x0 -> x1, Pallas kernels: none -> 148 us  [local(): pl.pallas_call(functools.partial(kernel, n_rows, n_cols, x_his), out_shap...]
    all_to_all x4 -> x0, waiting for transfers between devices: 76.4 us -> none  [the longest x2 56.3 us: sent_and_summed(): lax.all_to_all(pieces, axis, split_axis=0, concat_axis=0, tiled=True)]
    reduce_scatter x2 -> x0, waiting for transfers between devices: 43.9 us -> none  [local(): lax.psum_scatter(partial_rows(jnp.int32(0), own_rows * lax.axis_size('col...]
    all_to_all x4 -> x0, starting transfers between devices: 34.4 us -> none  [the longest x2 18 us: sent_and_summed(): lax.all_to_all(pieces, axis, split_axis=0, concat_axis=0, tiled=True)]
    dot_general x10 -> x0, matrix products: 29.4 us -> none  [the longest x2 17.1 us: partial_rows(): return jnp.dot(picked, chosen, preferred_element_type=jnp.float32)]
    gather x10 -> x0, local copies, waits for them, and re-layouts: 22.2 us -> none  [the longest x4 18.3 us: local(): picked = a_blocks[local_row[supernode][chosen_pos]]]
    convert_element_type x6 -> x0, local copies, waits for them, and re-layouts: 15.1 us -> none  [the longest x2 5.21 us: local(): chosen = chosen.astype(jnp.bfloat16).reshape(col_blocks * BS, panel_width)]
  transfers between devices with their start and end apart: 7 -> 0, of which waited for: 6 -> 0; matrix products, arithmetic and copies ran while one was open for 16% -> 0% of each run, Pallas kernels for 0% -> 0%
where the time goes in v1:
time: 159 us; the launch traced here: 158 us
  Pallas kernels  148 us (93%)
  local copies, waits for them, and re-layouts  4.99 us (3%)
  other arithmetic  4.11 us (3%)
    pallas_call x1, Pallas kernels, local(): pl.pallas_call(functools.partial(kernel, n_rows, n_cols, x_his), out_shap...  148 us
    unnamed x4, local copies, waits for them, and re-layouts  4.95 us

profile of v1, /device:TPU:1, one launch (start us, length us, event | category | flops | bytes accessed | tf_op | source)
XLA Modules:
  0.0 158.4 jit_solution(7635100117691941254)
XLA Ops:
  0.6 0.9 select_reduce_fusion.2
  1.5 0.0 copy-start
  1.6 0.2 convert_reduce_fusion
  1.8 0.4 select_reduce_fusion.1
  2.2 0.6 select_reduce_fusion
  2.9 0.6 pad_add_fusion.2.by_row
  3.6 0.6 pad_add_fusion.by_col
  4.3 0.6 pad_add_fusion.1.by_k
  4.9 0.0 copy-done
  4.9 148.5 %shard_map.59 = (f32[2,128,512]{2,1,0:T(8,128)}, f32[2,512,512]{2,1,0:T(8,128)}) custom-call(bf16[26,128,1664]{2,1,0:T(8,128)(2,1)} %bitcast.38, bf16[2,512,512]{2,1,0:T(8,128)(2,1)} %pan.1, s32[2,64]{1,0:T(2,128)} %copy-done, s32[3,2,16,16]{3,2,1,0:T(8,128)} %pad_add_fusion.by_col, s32[2,2,8,16]{3,2,1,0:T(8,128)} %pad_add_fusion.2.by_row, ...), custom_call_target="tpu_custom_call" | custom-call | tf_op jit(solution)/shard_map/pallas_call | solution.py:439
  153.4 1.9 %copy.8 = f32[2,128,512]{2,1,0:T(8,128)} copy(f32[2,128,512]{2,1,0:T(8,128)} %get-tuple-element.16) | data formatting | bytes 1048576
  155.3 3.1 %copy.9 = f32[2,512,512]{2,1,0:T(8,128)} copy(f32[2,512,512]{2,1,0:T(8,128)} %get-tuple-element.17) | data formatting | bytes 4194304
  (16 shorter events, 0.2 us)
Async XLA Ops:
  1.5 3.4 %copy-start = (s32[2,64]{1,0:T(2,128)}, s32[2,64]{1,0:T(2,128)S(1)}, u32[]{:S(2)}) copy-start(s32[2,64]{1,0:T(2,128)S(1)} %get-tuple-element.11.cols) | copy-start | bytes 1540

commit v2 on v1

--- a/solution.py
+++ b/solution.py
@@ -18,39 +18,31 @@
     ids = jnp.arange(n_blocks, dtype=jnp.int32)
     slots = jnp.sum(jnp.where(list_ids[..., None] == ids, block_slot, 0), axis=-1)
     col_blocks, row_blocks = n_blocks // n_cols, n_blocks // n_rows
-    col = slots // col_blocks
     row = slots // row_blocks
     pos = jnp.arange(listed, dtype=jnp.int32)
     before = pos[None, :] < pos[:, None]
-    rank = jnp.sum(((col[:, :, None] == col[:, None, :]) & before).astype(jnp.int32), axis=-1)
     kth = jnp.sum(((row[:, :, None] == row[:, None, :]) & before).astype(jnp.int32), axis=-1)
-    code = 1 + (slots * 16 + rank) * 64 + pos
-
-    def listed_in(group, index, groups):
-        to_group = group[:, None, None, :] == jnp.arange(groups, dtype=jnp.int32)[:, None, None]
-        to_index = index[:, None, None, :] == jnp.arange(16, dtype=jnp.int32)[:, None]
-        return jnp.sum(jnp.where(to_group & to_index, code[:, None, None, :], 0), axis=-1)
-
-    by_col = listed_in(col, rank, n_cols)
-    by_row = listed_in(row, kth, n_rows)
-    col_code, row_code = jnp.maximum(by_col - 1, 0), jnp.maximum(by_row - 1, 0)
+    key = row * n_cols + kth
+    keys = jnp.arange(n_rows * n_cols, dtype=jnp.int32)
+    code = jnp.sum(jnp.where(key[:, None, :] == keys[:, None], (1 + slots * listed + pos)[:, None, :], 0), axis=-1)
+    slot, place = jnp.maximum(code - 1, 0) // listed, jnp.maximum(code - 1, 0) % listed
     shard = listed // n_cols
-    col_table = jnp.stack([(by_col > 0).astype(jnp.int32), col_code % 64 // shard, col_code // 1024 % col_blocks])
-    row_table = jnp.stack([(by_row > 0).astype(jnp.int32), row_code // 1024 % row_blocks])
-    of_col = jnp.repeat(row_code, n_cols // n_rows, axis=1)
-    here = jnp.repeat(by_row, n_cols // n_rows, axis=1) > 0
-    here &= of_col // 1024 // col_blocks == jnp.arange(n_cols, dtype=jnp.int32)[:, None]
-    left_table = jnp.stack([here.astype(jnp.int32), jnp.where(here, of_col // 64 % 16, 0)])
-    return col, col_table, row_table, left_table
+    table = jnp.stack(
+        [
+            (code > 0).astype(jnp.int32), place // shard, slot // col_blocks, slot % col_blocks, slot % row_blocks,
+            slot // col_blocks % 2,
+        ]
+    )
+    return slots // col_blocks, table
 
 
 def kernel(
     n_rows, n_cols, x_his,
-    inv_hbm, pan, cols, by_col, by_row, by_k,
+    inv_hbm, pan, cols, by_k,
     out, diag,
-    a_all, a_pick, p_send, p_recv, ag_send, p_all, l_send, l_recv, m_send, left,
+    a_all, a_pick, p_send, p_recv, p_all, l_recv, left,
     part, core_recv, z_recv, x_recv, d_part, d_sib, d_row, d_row_in, d_col, d_col_in, e_piece, e_col, e_row,
-    a_sem, p_ss, p_rs, ag_ss, ag_rs, l_ss, l_rs, m_ss, m_rs, c_ss, c_rs, z_ss, z_rs, x_ss, x_rs,
+    a_sem, p_ss, p_rs, b_ss, b_rs, ag_ss, ag_rs, as_ss, as_rs, l_ss, l_rs, m_ss, m_rs, c_ss, c_rs, z_ss, z_rs, x_ss, x_rs,
     ds_ss, ds_rs, dr_ss, dr_rs, dc_ss, dc_rs, ec_ss, ec_rs, er_ss, er_rs, es_ss, es_rs,
 ):
     supers = pan.shape[0]
@@ -60,6 +52,7 @@
     width = pan.shape[2]
     chips = n_cols // 2
     zs = chips // x_his
+    ys = n_rows // 2
     me_r, me_c = lax.axis_index("row"), lax.axis_index("col")
     core = lax.rem(me_c, 2)
     chip = me_c // 2
@@ -102,60 +95,163 @@
             p_send[d, s] = pick_for(lax.rem(me_c + d, n_cols), s)
 
     for s in range(supers):
-        p_recv[me_c, s] = pick_for(me_c, s)
+        p_recv[core, me_c, s] = pick_for(me_c, s)
 
     pl.semaphore_wait(barrier, n_cols + n_rows - 2)
 
-    def p_copy(d):
-        return remote(p_send.at[d], p_recv.at[me_c], p_ss.at[d], p_rs.at[d], (me_r, lax.rem(me_c + d, n_cols)))
-
-    def p_arrive(d):
-        return remote(p_send.at[d], p_recv.at[lax.rem(me_c - d + n_cols, n_cols)], p_ss.at[d], p_rs.at[d], (me_r, lax.rem(me_c + d, n_cols)))
+    def p_copy(d, source):
+        to = (me_r, lax.rem(me_c + d, n_cols))
+        return remote(p_send.at[d], p_recv.at[lax.rem(to[1], 2), source], p_ss.at[d], p_rs.at[d], to)
 
     @pl.loop(1, n_cols)
     def _(d):
-        p_copy(d).start()
+        p_copy(d, me_c).start()
+
+    def picks(s):
+        @pl.loop(0, n_cols)
+        def _(i):
+            half_of, place = i // chips, lax.rem(i, chips)
+            k = 2 * place + jnp.where(half_of == 1, core, 1 - core)
+            a_row = by_k[4, s, me_r * n_cols + k]
+            rows = pl.ds(pl.multiple_of(i * BS, BS), BS)
+            for b in range(n_cols):
+                block = a_all[by_k[3, s, chip * n_cols + b], a_row]
+                here = by_k[0, s, chip * n_cols + b] * (by_k[2, s, chip * n_cols + b] == me_c) == 1
+                a_pick[s, rows, b * BS : (b + 1) * BS] = jnp.where(here, block, jnp.zeros_like(block))
+
+    @pl.loop(0, col_blocks)
+    def _(b):
+        load_a(b).wait()
+
+    picks(0)
 
     @pl.loop(1, n_cols)
     def _(d):
-        p_arrive(d).wait_recv()
-
-    def ag_copy(s, d):
-        return remote(ag_send.at[s], p_all.at[s, :, me_r], ag_ss.at[s, d], ag_rs.at[s, d], (lax.rem(me_r + d, n_rows), me_c))
-
-    def ag_arrive(s, d):
-        return remote(ag_send.at[s], p_all.at[s, :, lax.rem(me_r - d + n_rows, n_rows)], ag_ss.at[s, d], ag_rs.at[s, d], (lax.rem(me_r + d, n_rows), me_c))
-
-    for s in range(supers):
-        @pl.loop(0, col_blocks)
-        def _(i, s=s):
-            block = p_recv[by_col[1, s, me_c, i], s]
-            block = jnp.where(by_col[0, s, me_c, i] == 1, block, jnp.zeros_like(block))
-            ag_send[s, i] = block
-            p_all[s, i, me_r] = block
+        source = lax.rem(me_c - d + n_cols, n_cols)
+        remote(p_send.at[d], p_recv.at[core, source], p_ss.at[d], p_rs.at[d], sibling).wait_recv()
+
+    def b_copy(of):
+        return remote(p_recv.at[of], p_recv.at[of], b_ss, b_rs, sibling)
+
+    b_copy(core).start()
+    b_copy(1 - core).wait_recv()
+
+    mine = pl.ds(core * chips, chips)
+    x_lo, y = me_r // ys, lax.rem(me_r, ys)
+    up, down, across = x_lo * ys + lax.rem(y + 1, ys), x_lo * ys + lax.rem(y + ys - 1, ys), (1 - x_lo) * ys + y
+    far = x_lo * ys + lax.rem(y + 2, ys)
+    far_up, far_down = lax.rem(up + ys, n_rows), lax.rem(down + ys, n_rows)
+    far_far = lax.rem(far + ys, n_rows)
+    first = pl.ds(core * chips, chips // 2)
+    second = pl.ds(core * chips + chips // 2, chips // 2)
+
+    def ag_copy(s, j, slots, source, to):
+        block = p_all.at[s, slots, source]
+        return remote(block, block, ag_ss.at[s, j], ag_rs.at[s, j], (to, me_c))
+
+    sends = {
+        0: (mine, me_r, up), 1: (mine, me_r, down), 2: (mine, me_r, across),
+        3: (first, down, up), 4: (second, up, down), 5: (mine, across, up), 6: (mine, across, down), 7: (mine, far, across),
+    }
+    arrivals = {
+        0: (mine, down), 1: (mine, up), 2: (mine, across),
+        3: (first, far), 4: (second, far), 5: (mine, far_down), 6: (mine, far_up), 7: (mine, far_far),
+    }
+
+    def ag_start(s, j):
+        ag_copy(s, j, *sends[j]).start()
+
+    def ag_wait(s, j):
+        ag_copy(s, j, *arrivals[j], across).wait_recv()
+
+    def as_copy(s, source, of):
+        block = p_all.at[s, pl.ds(of * chips, chips), source]
+        return remote(block, block, as_ss.at[s, source], as_rs.at[s, source], sibling)
+
+    def pack(s):
+        for t in range(chips):
+            k = core * chips + t
+            block = p_recv[by_k[5, s, chip * n_cols + k], by_k[1, s, chip * n_cols + k], s]
+            valid = by_k[0, s, chip * n_cols + k] == 1
+            p_all[s, k, me_r] = jnp.where(valid, block, jnp.zeros_like(block))
+
+    def ag_first(s):
+        for j in (0, 1, 2):
+            ag_start(s, j)
+        as_copy(s, me_r, core).start()
+
+    def ag_second(s):
+        ag_wait(s, 2)
+        ag_start(s, 5)
+        ag_start(s, 6)
+        ag_wait(s, 0)
+        ag_start(s, 3)
+        ag_wait(s, 1)
+        ag_start(s, 4)
+        for source in (across, down, up):
+            as_copy(s, source, core).start()
+
+    def ag_third(s):
+        ag_wait(s, 3)
+        ag_wait(s, 4)
+        ag_start(s, 7)
+        ag_wait(s, 5)
+        ag_wait(s, 6)
+        for source in (far, far_down, far_up):
+            as_copy(s, source, core).start()
+        ag_wait(s, 7)
+        as_copy(s, far_far, core).start()
+
+    def l_copy(t):
+        k = core * chips + t
+        return remote(p_all.at[:, k, me_r], l_recv.at[chip], l_ss.at[t], l_rs.at[chip], (me_r, k))
+
+    def l_arrive(j):
+        return remote(p_all.at[:, 0, me_r], l_recv.at[j], l_ss.at[0], l_rs.at[j], sibling)
+
+    def l_first():
+        @pl.loop(0, chips)
+        def _(t):
+            k = core * chips + t
+
+            @pl.when(k != me_c)
+            def _():
+                l_copy(t).start()
+
+            @pl.when(k == me_c)
+            def _():
+                l_recv[chip] = p_all[:, k, me_r]
+
+    def m_copy(d):
+        g = lax.rem(me_r + d, n_rows)
+        return remote(l_recv.at[g], left.at[:, me_r], m_ss.at[d], m_rs.at[d], (g, me_c))
+
+    def m_arrive(d):
+        source = lax.rem(me_r - d + n_rows, n_rows)
+        return remote(l_recv.at[0], left.at[:, source], m_ss.at[d], m_rs.at[d], (source, me_c))
+
+    def l_second():
+        @pl.loop(0, chips)
+        def _(j):
+            @pl.when(2 * j + me_c // chips != me_c)
+            def _():
+                l_arrive(j).wait_recv()
+
+        left[:, me_r] = l_recv[me_r]
 
         @pl.loop(1, n_rows)
-        def _(d, s=s):
-            ag_copy(s, d).start()
-
-    def left_for(k, s):
-        block = ag_send[s, by_k[1, s, me_c, k]]
-        return jnp.where(by_k[0, s, me_c, k] == 1, block, jnp.zeros_like(block))
-
-    def l_copy(d):
-        return remote(l_send.at[d], l_recv.at[me_c], l_ss.at[d], l_rs.at[d], (me_r, lax.rem(me_c + d, n_cols)))
-
-    def l_arrive(d):
-        return remote(l_send.at[d], l_recv.at[lax.rem(me_c - d + n_cols, n_cols)], l_ss.at[d], l_rs.at[d], (me_r, lax.rem(me_c + d, n_cols)))
-
-    for s in range(supers):
-        l_recv[me_c, s] = left_for(me_c, s)
-
-    @pl.loop(1, n_cols)
-    def _(d):
-        for s in range(supers):
-            l_send[d, s] = left_for(lax.rem(me_c + d, n_cols), s)
-        l_copy(d).start()
+        def _(d):
+            m_copy(d).start()
+
+    pack(0)
+    ag_first(0)
+    pack(1)
+    picks(1)
+    ag_second(0)
+    ag_first(1)
+    l_first()
+    ag_third(0)
+    ag_second(1)
 
     def c_copy(s, h):
         return remote(part.at[s, 0, h], core_recv.at[s, h], c_ss.at[s, h], c_rs.at[s, h], sibling)
@@ -165,56 +261,30 @@
         return remote(part.at[s, 1, h, lax.rem(z + d, zs)], z_recv.at[s, h, d], z_ss.at[s, h, d], z_rs.at[s, h, d], to)
 
     def products(s):
-        @pl.loop(1, n_rows)
-        def _(d):
-            ag_arrive(s, d).wait_recv()
-
-        if s == 0:
-            @pl.loop(0, col_blocks)
-            def _(b):
-                load_a(b).wait()
+        @pl.loop(0, n_rows)
+        def _(source):
+            as_copy(s, source, 1 - core).wait_recv()
 
         @pl.loop(0, 2 * x_his)
         def _(i):
-            mine, h = i // x_his, lax.rem(i, x_his)
-            for u in range(zs):
-                k = 2 * (h * zs + u) + jnp.where(mine == 1, core, 1 - core)
-                a_row = by_row[1, s, me_r, k]
-                for b in range(col_blocks):
-                    a_pick[u * BS : (u + 1) * BS, b * BS : (b + 1) * BS] = a_all[by_col[2, s, me_c, b], a_row]
-            product = jnp.dot(a_pick[...], p_all[s].reshape(col_blocks * BS, width), preferred_element_type=F32)
-            part[s, mine, h] = product.reshape(zs, BS, width)
-
-            @pl.when(mine == 0)
+            half_of, h = i // x_his, lax.rem(i + 1 + x_hi, x_his)
+            rows = pl.ds(pl.multiple_of((half_of * chips + h * zs) * BS, BS), zs * BS)
+            product = jnp.dot(a_pick[s, rows, :], p_all[s].reshape(n_cols * BS, width), preferred_element_type=F32)
+            part[s, half_of, h] = product.reshape(zs, BS, width)
+
+            @pl.when(half_of == 0)
             def _():
                 c_copy(s, h).start()
 
-        for h in range(x_his):
+        for h in (1 - x_hi, x_hi):
             c_copy(s, h).wait_recv()
             part[s, 1, h] = part[s, 1, h] + core_recv[s, h]
             for d in range(1, zs):
                 z_copy(s, h, d).start()
 
-    def m_copy(d):
-        return remote(m_send.at[d], left.at[:, me_r], m_ss.at[d], m_rs.at[d], (lax.rem(me_r + d, n_rows), me_c))
-
-    def m_arrive(d):
-        return remote(m_send.at[d], left.at[:, lax.rem(me_r - d + n_rows, n_rows)], m_ss.at[d], m_rs.at[d], (lax.rem(me_r + d, n_rows), me_c))
-
     products(0)
-
-    @pl.loop(1, n_cols)
-    def _(d):
-        l_arrive(d).wait_recv()
-
-    left[:, me_r] = l_recv[2 * me_r] + l_recv[2 * me_r + 1]
-
-    @pl.loop(1, n_rows)
-    def _(d):
-        g = lax.rem(me_r + d, n_rows)
-        m_send[d] = l_recv[2 * g] + l_recv[2 * g + 1]
-        m_copy(d).start()
-
+    l_second()
+    ag_third(1)
     products(1)
 
     @pl.loop(1, n_rows)
@@ -267,7 +337,7 @@
     def finish_sums(s):
         x_copy(s).wait_recv()
         total = part[s, 1, x_hi, z] + x_recv[s]
-        valid = by_row[0, s, me_r, me_c] == 1
+        valid = by_k[0, s, me_r * n_cols + me_c] == 1
         total = jnp.where(valid, total, jnp.zeros_like(total))
         out[s] = total
         high = total.astype(BF16)
@@ -354,17 +424,30 @@
 
     @pl.loop(1, n_cols)
     def _(d):
-        p_copy(d).wait_send()
-        l_copy(d).wait_send()
+        p_copy(d, me_c).wait_send()
+
+    b_copy(core).wait_send()
+
+    @pl.loop(0, chips)
+    def _(t):
+        @pl.when(core * chips + t != me_c)
+        def _():
+            l_copy(t).wait_send()
 
     @pl.loop(1, n_rows)
     def _(d):
         m_copy(d).wait_send()
 
     for s in range(supers):
+        for j in sends:
+            ag_copy(s, j, *sends[j]).wait_send()
+
+        @pl.loop(0, n_rows)
+        def _(source, s=s):
+            as_copy(s, source, core).wait_send()
+
         @pl.loop(1, n_rows)
         def _(d, s=s):
-            ag_copy(s, d).wait_send()
             dr_copy(s, d).wait_send()
             er_copy(s, d, me_r).wait_send()
 
@@ -399,14 +482,11 @@
     dma = pltpu.SemaphoreType.DMA
     scratch = [
         pltpu.VMEM((col_blocks, blocks.shape[0], BS, BS), BF16),
-        pltpu.VMEM((zs * BS, col_blocks * BS), BF16),
+        pltpu.VMEM((supers, n_cols * BS, n_cols * BS), BF16),
         pltpu.VMEM((n_cols, supers, sub, width), BF16),
-        pltpu.VMEM((n_cols, supers, sub, width), BF16),
-        pltpu.VMEM((supers, col_blocks, sub, width), BF16),
-        pltpu.VMEM((supers, col_blocks, n_rows, sub, width), BF16),
-        pltpu.VMEM((n_cols, supers, sub, width), BF16),
-        pltpu.VMEM((n_cols, supers, sub, width), BF16),
-        pltpu.VMEM((n_rows, supers, sub, width), BF16),
+        pltpu.VMEM((2, n_cols, supers, sub, width), BF16),
+        pltpu.VMEM((supers, n_cols, n_rows, sub, width), BF16),
+        pltpu.VMEM((chips, supers, sub, width), BF16),
         pltpu.VMEM((supers, n_rows, sub, width), BF16),
         pltpu.VMEM((supers, 2, x_his, zs, BS, width), F32),
         pltpu.VMEM((supers, x_his, zs, BS, width), F32),
@@ -423,8 +503,10 @@
         pltpu.VMEM((supers, piece, width), F32),
         dma((col_blocks,)),
         dma((n_cols,)), dma((n_cols,)),
+        dma(()), dma(()),
+        dma((supers, 8)), dma((supers, 8)),
         dma((supers, n_rows)), dma((supers, n_rows)),
-        dma((n_cols,)), dma((n_cols,)),
+        dma((chips,)), dma((chips,)),
         dma((n_rows,)), dma((n_rows,)),
         dma((supers, x_his)), dma((supers, x_his)),
         dma((supers, x_his, zs)), dma((supers, x_his, zs)),
@@ -442,7 +524,7 @@
             jax.ShapeDtypeStruct((supers, BS, width), F32),
             jax.ShapeDtypeStruct((supers, width, width), F32),
         ),
-        in_specs=[pl.BlockSpec(memory_space=pl.ANY), vmem, smem, smem, smem, smem],
+        in_specs=[pl.BlockSpec(memory_space=pl.ANY), vmem, smem, smem],
         out_specs=(vmem, vmem),
         scratch_shapes=scratch,
         compiler_params=pltpu.CompilerParams(

time: 159 us -> 133 us (0.84)
  Pallas kernels: 148 us -> 124 us
  other arithmetic: 4.11 us -> 1.89 us
    pallas_call x1, Pallas kernels: 148 us -> 124 us  [local(): pl.pallas_call(functools.partial(kernel, n_rows, n_cols, x_his), out_shap...]
    another operation x3 -> x1, other arithmetic: 1.85 us -> 0.03 us  [tables(): jnp.stack([(code > 0).astype(jnp.int32), place // shard, slot // col_bloc...]
where the time goes in v2:
time: 133 us; the launch traced here: 132 us
  Pallas kernels  124 us (93%)
  local copies, waits for them, and re-layouts  5.54 us (4%)
  other arithmetic  1.89 us (1%)
    pallas_call x1, Pallas kernels, local(): pl.pallas_call(functools.partial(kernel, n_rows, n_cols, x_his), out_shap...  124 us
    unnamed x4, local copies, waits for them, and re-layouts  5.54 us

profile of v2, /device:TPU:1, one launch (start us, length us, event | category | flops | bytes accessed | tf_op | source)
XLA Modules:
  0.0 132.4 jit_solution(12485281103173224915)
XLA Ops:
  0.6 0.9 select_reduce_fusion
  1.5 0.6 and_select_fusion.6
  2.1 0.2 convert_reduce_fusion
  2.3 0.1 select_reduce_fusion.1
  2.5 0.0 copy-start
  2.6 0.6 copy-done
  3.1 124.3 %shard_map.59 = (f32[2,128,512]{2,1,0:T(8,128)}, f32[2,512,512]{2,1,0:T(8,128)}) custom-call(bf16[26,128,1664]{2,1,0:T(8,128)(2,1)} %bitcast.50, bf16[2,512,512]{2,1,0:T(8,128)(2,1)} %pan.1, s32[2,64]{1,0:T(2,128)} %get-tuple-element.3.cols, s32[6,2,128]{2,1,0:T(2,128)} %copy-done), custom_call_target="tpu_custom_call" | custom-call | tf_op jit(solution)/shard_map/pallas_call | solution.py:521
  127.4 1.9 %copy.13 = f32[2,128,512]{2,1,0:T(8,128)} copy(f32[2,128,512]{2,1,0:T(8,128)} %get-tuple-element.7) | data formatting | bytes 1048576
  129.3 3.1 %copy.14 = f32[2,512,512]{2,1,0:T(8,128)} copy(f32[2,512,512]{2,1,0:T(8,128)} %get-tuple-element.8) | data formatting | bytes 4194304
  (8 shorter events, 0.1 us)
Async XLA Ops:
  2.5 0.6 copy-start

commit v3 on v2

--- a/solution.py
+++ b/solution.py
@@ -36,12 +36,30 @@
     return slots // col_blocks, table
 
 
+SCALE_ROWS = 16
+TOP = 32000.0
+
+
+def encode(ref, block):
+    top = jnp.max(jnp.abs(block), axis=0, keepdims=True)
+    exponent = jnp.floor(jnp.log2(jnp.maximum(top, 1e-30))) + 1.0
+    coded = jnp.round(block * (jnp.exp2(-exponent) * TOP))
+    ref[0:BS] = coded.astype(jnp.int32).astype(jnp.int16)
+    exponents = jnp.broadcast_to(exponent, (SCALE_ROWS, block.shape[1]))
+    ref[BS : BS + SCALE_ROWS] = exponents.astype(jnp.int32).astype(jnp.int16)
+
+
+def decode(ref):
+    exponent = ref[BS : BS + SCALE_ROWS].astype(jnp.int32).astype(F32)[0:1]
+    return ref[0:BS].astype(jnp.int32).astype(F32) * (jnp.exp2(exponent) * (1.0 / TOP))
+
+
 def kernel(
     n_rows, n_cols, x_his,
     inv_hbm, pan, cols, by_k,
     out, diag,
     a_all, a_pick, p_send, p_recv, p_all, l_recv, left,
-    part, core_recv, z_recv, x_recv, d_part, d_sib, d_row, d_row_in, d_col, d_col_in, e_piece, e_col, e_row,
+    part, core_recv, z_send, z_recv, x_send, x_recv, d_part, d_sib, d_row, d_row_in, d_col, d_col_in, e_piece, e_col, e_row,
     a_sem, p_ss, p_rs, b_ss, b_rs, ag_ss, ag_rs, as_ss, as_rs, l_ss, l_rs, m_ss, m_rs, c_ss, c_rs, z_ss, z_rs, x_ss, x_rs,
     ds_ss, ds_rs, dr_ss, dr_rs, dc_ss, dc_rs, ec_ss, ec_rs, er_ss, er_rs, es_ss, es_rs,
 ):
@@ -258,7 +276,7 @@
 
     def z_copy(s, h, d):
         to = (me_r, (x_hi * zs + lax.rem(z + d, zs)) * 2 + core)
-        return remote(part.at[s, 1, h, lax.rem(z + d, zs)], z_recv.at[s, h, d], z_ss.at[s, h, d], z_rs.at[s, h, d], to)
+        return remote(z_send.at[s, h, d], z_recv.at[s, h, d], z_ss.at[s, h, d], z_rs.at[s, h, d], to)
 
     def products(s):
         @pl.loop(0, n_rows)
@@ -278,8 +296,11 @@
 
         for h in (1 - x_hi, x_hi):
             c_copy(s, h).wait_recv()
-            part[s, 1, h] = part[s, 1, h] + core_recv[s, h]
-            for d in range(1, zs):
+
+            @pl.loop(1, zs)
+            def _(d, h=h):
+                there = lax.rem(z + d, zs)
+                encode(z_send.at[s, h, d], part[s, 1, h, there] + core_recv[s, h, there])
                 z_copy(s, h, d).start()
 
     products(0)
@@ -293,14 +314,18 @@
 
     def x_copy(s):
         to = (me_r, ((1 - x_hi) * zs + z) * 2 + core)
-        return remote(part.at[s, 1, 1 - x_hi, z], x_recv.at[s], x_ss.at[s], x_rs.at[s], to)
+        return remote(x_send.at[s], x_recv.at[s], x_ss.at[s], x_rs.at[s], to)
 
     def over_z(s, h):
-        total = part[s, 1, h, z]
+        total = part[s, 1, h, z] + core_recv[s, h, z]
         for d in range(1, zs):
             z_copy(s, h, d).wait_recv()
-            total = total + z_recv[s, h, d]
-        part[s, 1, h, z] = total
+            total = total + decode(z_recv.at[s, h, d])
+        return total
+
+    def start_x(s):
+        encode(x_send.at[s], over_z(s, 1 - x_hi))
+        x_copy(s).start()
 
     half = width // 2
     piece = half // n_rows
@@ -335,8 +360,9 @@
         return remote(diag.at[s, there], diag.at[s, there], es_ss.at[s], es_rs.at[s], sibling)
 
     def finish_sums(s):
+        total = over_z(s, x_hi)
         x_copy(s).wait_recv()
-        total = part[s, 1, x_hi, z] + x_recv[s]
+        total = total + decode(x_recv.at[s])
         valid = by_k[0, s, me_r * n_cols + me_c] == 1
         total = jnp.where(valid, total, jnp.zeros_like(total))
         out[s] = total
@@ -403,14 +429,10 @@
 
         es_copy(s, core).start()
 
-    over_z(0, 1 - x_hi)
-    x_copy(0).start()
-    over_z(0, x_hi)
+    start_x(0)
     finish_sums(0)
     over_cores(0)
-    over_z(1, 1 - x_hi)
-    x_copy(1).start()
-    over_z(1, x_hi)
+    start_x(1)
     over_rows(0)
     finish_sums(1)
     over_cores(1)
@@ -490,8 +512,10 @@
         pltpu.VMEM((supers, n_rows, sub, width), BF16),
         pltpu.VMEM((supers, 2, x_his, zs, BS, width), F32),
         pltpu.VMEM((supers, x_his, zs, BS, width), F32),
-        pltpu.VMEM((supers, x_his, zs, BS, width), F32),
-        pltpu.VMEM((supers, BS, width), F32),
+        pltpu.VMEM((supers, x_his, zs, BS + SCALE_ROWS, width), jnp.int16),
+        pltpu.VMEM((supers, x_his, zs, BS + SCALE_ROWS, width), jnp.int16),
+        pltpu.VMEM((supers, BS + SCALE_ROWS, width), jnp.int16),
+        pltpu.VMEM((supers, BS + SCALE_ROWS, width), jnp.int16),
         pltpu.VMEM((supers, width, width), F32),
         pltpu.VMEM((supers, half, width), F32),
         pltpu.VMEM((supers, n_rows, piece, width), F32),

time: 133 us -> 123 us (0.925)
  Pallas kernels: 124 us -> 114 us
    pallas_call x1, Pallas kernels: 124 us -> 114 us  [local(): pl.pallas_call(functools.partial(kernel, n_rows, n_cols, x_his), out_shap...]
where the time goes in v3:
time: 123 us; the launch traced here: 122 us
  Pallas kernels  114 us (93%)
  local copies, waits for them, and re-layouts  5.54 us (5%)
  other arithmetic  1.89 us (2%)
    pallas_call x1, Pallas kernels, local(): pl.pallas_call(functools.partial(kernel, n_rows, n_cols, x_his), out_shap...  114 us
    unnamed x4, local copies, waits for them, and re-layouts  5.54 us

profile of v3, /device:TPU:1, one launch (start us, length us, event | category | flops | bytes accessed | tf_op | source)
XLA Modules:
  0.0 122.4 jit_solution(15461513681232803558)
XLA Ops:
  0.6 0.9 select_reduce_fusion
  1.5 0.6 and_select_fusion.6
  2.1 0.2 convert_reduce_fusion
  2.3 0.1 select_reduce_fusion.1
  2.5 0.0 copy-start
  2.6 0.6 copy-done
  3.1 114.3 %shard_map.59 = (f32[2,128,512]{2,1,0:T(8,128)}, f32[2,512,512]{2,1,0:T(8,128)}) custom-call(bf16[26,128,1664]{2,1,0:T(8,128)(2,1)} %bitcast.50, bf16[2,512,512]{2,1,0:T(8,128)(2,1)} %pan.1, s32[2,64]{1,0:T(2,128)} %get-tuple-element.3.cols, s32[6,2,128]{2,1,0:T(2,128)} %copy-done), custom_call_target="tpu_custom_call" | custom-call | tf_op jit(solution)/shard_map/pallas_call | solution.py:545
  117.4 1.9 %copy.13 = f32[2,128,512]{2,1,0:T(8,128)} copy(f32[2,128,512]{2,1,0:T(8,128)} %get-tuple-element.7) | data formatting | bytes 1048576
  119.3 3.1 %copy.14 = f32[2,512,512]{2,1,0:T(8,128)} copy(f32[2,512,512]{2,1,0:T(8,128)} %get-tuple-element.8) | data formatting | bytes 4194304
  (8 shorter events, 0.1 us)
Async XLA Ops:
  2.5 0.6 copy-start

commit v4 on v3

--- a/solution.py
+++ b/solution.py
@@ -58,12 +58,13 @@
     n_rows, n_cols, x_his,
     inv_hbm, pan, cols, by_k,
     out, diag,
-    a_all, a_pick, p_send, p_recv, p_all, l_recv, left,
-    part, core_recv, z_send, z_recv, x_send, x_recv, d_part, d_sib, d_row, d_row_in, d_col, d_col_in, e_piece, e_col, e_row,
+    a_all, a_pick, p_send, p_recv_0, p_recv_1, p_all, l_recv, left,
+    part, core_recv, z_send, z_recv, x_send, x_recv, d_part, d_sib, u_send, u_recv, v_send, v_recv, t_all,
     a_sem, p_ss, p_rs, b_ss, b_rs, ag_ss, ag_rs, as_ss, as_rs, l_ss, l_rs, m_ss, m_rs, c_ss, c_rs, z_ss, z_rs, x_ss, x_rs,
-    ds_ss, ds_rs, dr_ss, dr_rs, dc_ss, dc_rs, ec_ss, ec_rs, er_ss, er_rs, es_ss, es_rs,
+    ds_ss, ds_rs, u_ss, u_rs, v_ss, v_rs, t_ss, t_rs, w_ss, w_rs, er_ss, er_rs, es_ss, es_rs,
 ):
     supers = pan.shape[0]
+    p_recv = (p_recv_0, p_recv_1)
     sub = BS // n_rows
     col_blocks = a_all.shape[0]
     shard = pan.shape[1] // BS
@@ -100,6 +101,9 @@
     def _(d):
         pl.semaphore_signal(barrier, inc=1, device_id=(lax.rem(me_r + d, n_rows), me_c), device_id_type=MESH)
 
+    opposite = (lax.rem(me_r + ys, n_rows), lax.rem(me_c + zs * 2, n_cols))
+    pl.semaphore_signal(barrier, inc=1, device_id=opposite, device_id_type=MESH)
+
     def pick_for(c, s):
         piece = jnp.zeros((sub, width), BF16)
         for q in range(shard):
@@ -110,20 +114,21 @@
     @pl.loop(1, n_cols)
     def _(d):
         for s in range(supers):
-            p_send[d, s] = pick_for(lax.rem(me_c + d, n_cols), s)
+            p_send[s, d] = pick_for(lax.rem(me_c + d, n_cols), s)
 
     for s in range(supers):
-        p_recv[core, me_c, s] = pick_for(me_c, s)
-
-    pl.semaphore_wait(barrier, n_cols + n_rows - 2)
-
-    def p_copy(d, source):
+        p_recv[s][core, me_c] = pick_for(me_c, s)
+
+    pl.semaphore_wait(barrier, n_cols + n_rows - 1)
+
+    def p_copy(s, d, source):
         to = (me_r, lax.rem(me_c + d, n_cols))
-        return remote(p_send.at[d], p_recv.at[lax.rem(to[1], 2), source], p_ss.at[d], p_rs.at[d], to)
-
-    @pl.loop(1, n_cols)
-    def _(d):
-        p_copy(d, me_c).start()
+        return remote(p_send.at[s, d], p_recv[s].at[lax.rem(to[1], 2), source], p_ss.at[s, d], p_rs.at[s, d], to)
+
+    for s in range(supers):
+        @pl.loop(1, n_cols)
+        def _(d, s=s):
+            p_copy(s, d, me_c).start()
 
     def picks(s):
         @pl.loop(0, n_cols)
@@ -143,16 +148,17 @@
 
     picks(0)
 
-    @pl.loop(1, n_cols)
-    def _(d):
-        source = lax.rem(me_c - d + n_cols, n_cols)
-        remote(p_send.at[d], p_recv.at[core, source], p_ss.at[d], p_rs.at[d], sibling).wait_recv()
-
-    def b_copy(of):
-        return remote(p_recv.at[of], p_recv.at[of], b_ss, b_rs, sibling)
-
-    b_copy(core).start()
-    b_copy(1 - core).wait_recv()
+    def b_copy(s, of):
+        return remote(p_recv[s].at[of], p_recv[s].at[of], b_ss.at[s], b_rs.at[s], sibling)
+
+    def to_cores(s):
+        @pl.loop(1, n_cols)
+        def _(d):
+            source = lax.rem(me_c - d + n_cols, n_cols)
+            remote(p_send.at[s, d], p_recv[s].at[core, source], p_ss.at[s, d], p_rs.at[s, d], sibling).wait_recv()
+
+        b_copy(s, core).start()
+        b_copy(s, 1 - core).wait_recv()
 
     mine = pl.ds(core * chips, chips)
     x_lo, y = me_r // ys, lax.rem(me_r, ys)
@@ -189,7 +195,7 @@
     def pack(s):
         for t in range(chips):
             k = core * chips + t
-            block = p_recv[by_k[5, s, chip * n_cols + k], by_k[1, s, chip * n_cols + k], s]
+            block = p_recv[s][by_k[5, s, chip * n_cols + k], by_k[1, s, chip * n_cols + k]]
             valid = by_k[0, s, chip * n_cols + k] == 1
             p_all[s, k, me_r] = jnp.where(valid, block, jnp.zeros_like(block))
 
@@ -261,10 +267,12 @@
         def _(d):
             m_copy(d).start()
 
+    to_cores(0)
     pack(0)
     ag_first(0)
+    picks(1)
+    to_cores(1)
     pack(1)
-    picks(1)
     ag_second(0)
     ag_first(1)
     l_first()
@@ -276,7 +284,7 @@
 
     def z_copy(s, h, d):
         to = (me_r, (x_hi * zs + lax.rem(z + d, zs)) * 2 + core)
-        return remote(z_send.at[s, h, d], z_recv.at[s, h, d], z_ss.at[s, h, d], z_rs.at[s, h, d], to)
+        return remote(z_send.at[s, h, d - 1], z_recv.at[s, h, d - 1], z_ss.at[s, h, d], z_rs.at[s, h, d], to)
 
     def products(s):
         @pl.loop(0, n_rows)
@@ -300,7 +308,7 @@
             @pl.loop(1, zs)
             def _(d, h=h):
                 there = lax.rem(z + d, zs)
-                encode(z_send.at[s, h, d], part[s, 1, h, there] + core_recv[s, h, there])
+                encode(z_send.at[s, h, d - 1], part[s, 1, h, there] + core_recv[s, h, there])
                 z_copy(s, h, d).start()
 
     products(0)
@@ -320,7 +328,7 @@
         total = part[s, 1, h, z] + core_recv[s, h, z]
         for d in range(1, zs):
             z_copy(s, h, d).wait_recv()
-            total = total + decode(z_recv.at[s, h, d])
+            total = total + decode(z_recv.at[s, h, d - 1])
         return total
 
     def start_x(s):
@@ -328,36 +336,50 @@
         x_copy(s).start()
 
     half = width // 2
-    piece = half // n_rows
+    ring = zs
+    piece, bit = half // ring, half // ring // ring
+    x_at = x_hi * 2 + x_lo
 
     def ds_copy(s):
         there = pl.ds(pl.multiple_of((1 - core) * half, half), half)
         return remote(d_part.at[s, there], d_sib.at[s], ds_ss.at[s], ds_rs.at[s], sibling)
 
-    def dr_copy(s, d):
-        g = lax.rem(me_r + d, n_rows)
-        return remote(d_row.at[s, g], d_row_in.at[s, d], dr_ss.at[s, d], dr_rs.at[s, d], (g, me_c))
-
-    def chip_at(d):
-        return lax.rem(chip + d, chips)
-
-    def dc_copy(s, d):
-        t = chip_at(d)
-        return remote(d_col.at[s, t], d_col_in.at[s, d], dc_ss.at[s, d], dc_rs.at[s, d], (me_r, 2 * t + core))
-
-    def ec_copy(s, d, source):
-        return remote(e_piece.at[s], e_col.at[s, source], ec_ss.at[s, d], ec_rs.at[s, d], (me_r, 2 * chip_at(d) + core))
-
-    def rows_of(r):
-        return pl.ds(pl.multiple_of(core * half + r * piece, piece), piece)
-
-    def er_copy(s, d, source):
-        to = (lax.rem(me_r + d, n_rows), me_c)
-        return remote(e_row.at[s], diag.at[s, rows_of(source)], er_ss.at[s, d], er_rs.at[s, d], to)
-
-    def es_copy(s, half_of):
-        there = pl.ds(pl.multiple_of(half_of * half, half), half)
-        return remote(diag.at[s, there], diag.at[s, there], es_ss.at[s], es_rs.at[s], sibling)
+    def place_in(f, step):
+        return y if f == step else z
+
+    def peer_at(f, step, d):
+        if step == 2:
+            peer = lax.rem(x_at + d, ring)
+            return peer, (lax.rem(peer, 2) * ys + y, ((peer // 2) * zs + z) * 2 + core)
+        peer = lax.rem(place_in(f, step) + d, ring)
+        return peer, (x_lo * ys + peer, me_c) if f == step else (me_r, (x_hi * zs + peer) * 2 + core)
+
+    def u_copy(s, f, d):
+        peer, to = peer_at(f, 0, d)
+        return remote(u_send.at[s, f, peer], u_recv.at[s, f, d], u_ss.at[s, f, d], u_rs.at[s, f, d], to)
+
+    def v_copy(s, f, d):
+        peer, to = peer_at(f, 1, d)
+        return remote(v_send.at[s, f, peer], v_recv.at[s, f, d], v_ss.at[s, f, d], v_rs.at[s, f, d], to)
+
+    def t_copy(s, f, d, source):
+        block = t_all.at[s, f, source]
+        return remote(block, block, t_ss.at[s, f, d], t_rs.at[s, f, d], peer_at(f, 2, d)[1])
+
+    def block_of(s, f, first, rows):
+        return diag.at[s, pl.ds(pl.multiple_of(first, rows), rows), f * half : (f + 1) * half]
+
+    def w_copy(s, f, d, source):
+        block = block_of(s, f, core * half + place_in(f, 0) * piece + source * bit, bit)
+        return remote(block, block, w_ss.at[s, f, d], w_rs.at[s, f, d], peer_at(f, 1, d)[1])
+
+    def er_copy(s, f, d, source):
+        block = block_of(s, f, core * half + source * piece, piece)
+        return remote(block, block, er_ss.at[s, f, d], er_rs.at[s, f, d], peer_at(f, 0, d)[1])
+
+    def es_copy(s, f, of):
+        block = block_of(s, f, of * half, half)
+        return remote(block, block, es_ss.at[s, f], es_rs.at[s, f], sibling)
 
     def finish_sums(s):
         total = over_z(s, x_hi)
@@ -366,89 +388,96 @@
         valid = by_k[0, s, me_r * n_cols + me_c] == 1
         total = jnp.where(valid, total, jnp.zeros_like(total))
         out[s] = total
+        total = -total
         high = total.astype(BF16)
         low = (total - high.astype(F32)).astype(BF16)
-        block = left[s].reshape(BS, width)
         contract = functools.partial(
             lax.dot_general, dimension_numbers=(((0,), (0,)), ((), ())), preferred_element_type=F32
         )
-        d_part[s] = -(contract(block, high) + contract(block, low))
-        ds_copy(s).start()
+        for of in (1 - core, core):
+            columns = pl.ds(pl.multiple_of(of * half, half), half)
+            block = left[s, :, :, columns].reshape(BS, half)
+            d_part[s, columns] = contract(block, high) + contract(block, low)
+            if of is not core:
+                ds_copy(s).start()
 
     def over_cores(s):
         ds_copy(s).wait_recv()
         here = pl.ds(pl.multiple_of(core * half, half), half)
-        total = d_part[s, here] + d_sib[s]
-        d_row[s] = total.reshape(n_rows, piece, width)
-
-        @pl.loop(1, n_rows)
-        def _(d):
-            dr_copy(s, d).start()
-
-    def over_rows(s):
-        total = d_row[s, me_r]
-        for d in range(1, n_rows):
-            dr_copy(s, d).wait_recv()
-            total = total + d_row_in[s, d]
-        for t in range(chips):
-            d_col[s, t] = total[(t // 2) * 8 : (t // 2) * 8 + 8, (t % 2) * half : (t % 2) * half + half]
-
-        @pl.loop(1, chips)
-        def _(d):
-            dc_copy(s, d).start()
-
-    def over_chips(s):
-        total = d_col[s, chip]
-        for d in range(1, chips):
-            dc_copy(s, d).wait_recv()
-            total = total + d_col_in[s, d]
-        e_piece[s] = total
-        e_col[s, chip] = total
-
-        @pl.loop(1, chips)
-        def _(d):
-            ec_copy(s, d, chip).start()
-
-    def back_over_chips(s):
-        @pl.loop(1, chips)
-        def _(d):
-            ec_copy(s, d, lax.rem(chip - d + chips, chips)).wait_recv()
-
-        for t in range(chips):
-            e_row[s, (t // 2) * 8 : (t // 2) * 8 + 8, (t % 2) * half : (t % 2) * half + half] = e_col[s, t]
-        diag[s, rows_of(me_r)] = e_row[s]
-
-        @pl.loop(1, n_rows)
-        def _(d):
-            er_copy(s, d, me_r).start()
-
-    def back_over_rows(s):
-        @pl.loop(1, n_rows)
-        def _(d):
-            er_copy(s, d, lax.rem(me_r - d + n_rows, n_rows)).wait_recv()
-
-        es_copy(s, core).start()
+        total = (d_part[s, here] + d_sib[s]).reshape(ring, piece, width)
+        for f in range(2):
+            u_send[s, f] = total[:, :, f * half : (f + 1) * half]
+            for d in range(1, ring):
+                u_copy(s, f, d).start()
+
+    def over_first(s):
+        for f in range(2):
+            total = u_send[s, f, place_in(f, 0)]
+            for d in range(1, ring):
+                u_copy(s, f, d).wait_recv()
+                total = total + u_recv[s, f, d]
+            v_send[s, f] = total.reshape(ring, bit, half)
+            for d in range(1, ring):
+                v_copy(s, f, d).start()
+
+    def over_second(s):
+        for f in range(2):
+            total = v_send[s, f, place_in(f, 1)]
+            for d in range(1, ring):
+                v_copy(s, f, d).wait_recv()
+                total = total + v_recv[s, f, d]
+            t_all[s, f, x_at] = total
+            for d in range(1, ring):
+                t_copy(s, f, d, x_at).start()
+
+    def over_third(s):
+        for f in range(2):
+            for d in range(1, ring):
+                t_copy(s, f, d, lax.rem(x_at - d + ring, ring)).wait_recv()
+            total = t_all[s, f, 0]
+            for x in range(1, ring):
+                total = total + t_all[s, f, x]
+            first = core * half + place_in(f, 0) * piece + place_in(f, 1) * bit
+            diag[s, pl.ds(pl.multiple_of(first, bit), bit), f * half : (f + 1) * half] = total
+            for d in range(1, ring):
+                w_copy(s, f, d, place_in(f, 1)).start()
+
+    def back_second(s):
+        for f in range(2):
+            for d in range(1, ring):
+                w_copy(s, f, d, lax.rem(place_in(f, 1) - d + ring, ring)).wait_recv()
+            for d in range(1, ring):
+                er_copy(s, f, d, place_in(f, 0)).start()
+
+    def back_first(s):
+        for f in range(2):
+            for d in range(1, ring):
+                er_copy(s, f, d, lax.rem(place_in(f, 0) - d + ring, ring)).wait_recv()
+            es_copy(s, f, core).start()
 
     start_x(0)
     finish_sums(0)
     over_cores(0)
     start_x(1)
-    over_rows(0)
+    over_first(0)
     finish_sums(1)
+    over_second(0)
     over_cores(1)
-    over_chips(0)
-    over_rows(1)
-    back_over_chips(0)
-    over_chips(1)
-    back_over_rows(0)
-    back_over_chips(1)
-    back_over_rows(1)
-
-    @pl.loop(1, n_cols)
-    def _(d):
-        p_copy(d, me_c).wait_send()
-
-    b_copy(core).wait_send()
+    over_third(0)
+    over_first(1)
+    back_second(0)
+    over_second(1)
+    back_first(0)
+    over_third(1)
+    back_second(1)
+    back_first(1)
+
+    for s in range(supers):
+        @pl.loop(1, n_cols)
+        def _(d, s=s):
+            p_copy(s, d, me_c).wait_send()
+
+        b_copy(s, core).wait_send()
 
     @pl.loop(0, chips)
     def _(t):
@@ -468,15 +497,16 @@
         def _(source, s=s):
             as_copy(s, source, core).wait_send()
 
-        @pl.loop(1, n_rows)
-        def _(d, s=s):
-            dr_copy(s, d).wait_send()
-            er_copy(s, d, me_r).wait_send()
-
-        @pl.loop(1, chips)
-        def _(d, s=s):
-            dc_copy(s, d).wait_send()
-            ec_copy(s, d, chip).wait_send()
+        for f in range(2):
+            for d in range(1, ring):
+                u_copy(s, f, d).wait_send()
+                v_copy(s, f, d).wait_send()
+                t_copy(s, f, d, x_at).wait_send()
+                w_copy(s, f, d, place_in(f, 1)).wait_send()
+                er_copy(s, f, d, place_in(f, 0)).wait_send()
+
+            es_copy(s, f, core).wait_send()
+            es_copy(s, f, 1 - core).wait_recv()
 
         for h in range(x_his):
             c_copy(s, h).wait_send()
@@ -484,8 +514,6 @@
                 z_copy(s, h, d).wait_send()
         x_copy(s).wait_send()
         ds_copy(s).wait_send()
-        es_copy(s, core).wait_send()
-        es_copy(s, 1 - core).wait_recv()
 
 
 def local(n_rows, n_cols, inverse, panels, block_slot, list_ids):
@@ -496,7 +524,6 @@
     chips = n_cols // 2
     zs = chips // x_his
     half = width // 2
-    piece = half // n_rows
     lists = tables(block_slot, list_ids, n_rows, n_cols)
     blocks = inverse.reshape(-1, BS, inverse.shape[1])
     vmem = pl.BlockSpec(memory_space=pltpu.VMEM)
@@ -505,29 +532,28 @@
     scratch = [
         pltpu.VMEM((col_blocks, blocks.shape[0], BS, BS), BF16),
         pltpu.VMEM((supers, n_cols * BS, n_cols * BS), BF16),
-        pltpu.VMEM((n_cols, supers, sub, width), BF16),
-        pltpu.VMEM((2, n_cols, supers, sub, width), BF16),
+        pltpu.VMEM((supers, n_cols, sub, width), BF16),
+        pltpu.VMEM((2, n_cols, sub, width), BF16),
+        pltpu.VMEM((2, n_cols, sub, width), BF16),
         pltpu.VMEM((supers, n_cols, n_rows, sub, width), BF16),
         pltpu.VMEM((chips, supers, sub, width), BF16),
         pltpu.VMEM((supers, n_rows, sub, width), BF16),
         pltpu.VMEM((supers, 2, x_his, zs, BS, width), F32),
         pltpu.VMEM((supers, x_his, zs, BS, width), F32),
-        pltpu.VMEM((supers, x_his, zs, BS + SCALE_ROWS, width), jnp.int16),
-        pltpu.VMEM((supers, x_his, zs, BS + SCALE_ROWS, width), jnp.int16),
+        pltpu.VMEM((supers, x_his, zs - 1, BS + SCALE_ROWS, width), jnp.int16),
+        pltpu.VMEM((supers, x_his, zs - 1, BS + SCALE_ROWS, width), jnp.int16),
         pltpu.VMEM((supers, BS + SCALE_ROWS, width), jnp.int16),
         pltpu.VMEM((supers, BS + SCALE_ROWS, width), jnp.int16),
         pltpu.VMEM((supers, width, width), F32),
         pltpu.VMEM((supers, half, width), F32),
-        pltpu.VMEM((supers, n_rows, piece, width), F32),
-        pltpu.VMEM((supers, n_rows, piece, width), F32),
-        pltpu.VMEM((supers, chips, 8, half), F32),
-        pltpu.VMEM((supers, chips, 8, half), F32),
-        pltpu.VMEM((supers, 8, half), F32),
-        pltpu.VMEM((supers, chips, 8, half), F32),
-        pltpu.VMEM((supers, piece, width), F32),
+        pltpu.VMEM((supers, 2, zs, half // zs, half), F32),
+        pltpu.VMEM((supers, 2, zs, half // zs, half), F32),
+        pltpu.VMEM((supers, 2, zs, half // zs // zs, half), F32),
+        pltpu.VMEM((supers, 2, zs, half // zs // zs, half), F32),
+        pltpu.VMEM((supers, 2, zs, half // zs // zs, half), F32),
         dma((col_blocks,)),
-        dma((n_cols,)), dma((n_cols,)),
-        dma(()), dma(()),
+        dma((supers, n_cols)), dma((supers, n_cols)),
+        dma((supers,)), dma((supers,)),
         dma((supers, 8)), dma((supers, 8)),
         dma((supers, n_rows)), dma((supers, n_rows)),
         dma((chips,)), dma((chips,)),
@@ -536,11 +562,12 @@
         dma((supers, x_his, zs)), dma((supers, x_his, zs)),
         dma((supers,)), dma((supers,)),
         dma((supers,)), dma((supers,)),
-        dma((supers, n_rows)), dma((supers, n_rows)),
-        dma((supers, chips)), dma((supers, chips)),
-        dma((supers, chips)), dma((supers, chips)),
-        dma((supers, n_rows)), dma((supers, n_rows)),
-        dma((supers,)), dma((supers,)),
+        dma((supers, 2, zs)), dma((supers, 2, zs)),
+        dma((supers, 2, zs)), dma((supers, 2, zs)),
+        dma((supers, 2, zs)), dma((supers, 2, zs)),
+        dma((supers, 2, zs)), dma((supers, 2, zs)),
+        dma((supers, 2, zs)), dma((supers, 2, zs)),
+        dma((supers, 2)), dma((supers, 2)),
     ]
     return pl.pallas_call(
         functools.partial(kernel, n_rows, n_cols, x_his),

time: 123 us -> 114 us (0.927)
  Pallas kernels: 114 us -> 106 us
    pallas_call x1, Pallas kernels: 114 us -> 106 us  [local(): pl.pallas_call(functools.partial(kernel, n_rows, n_cols, x_his), out_shap...]
where the time goes in v4:
time: 114 us
  Pallas kernels  106 us (93%)
  local copies, waits for them, and re-layouts  5.54 us (5%)
  other arithmetic  1.89 us (2%)
    pallas_call x1, Pallas kernels, local(): pl.pallas_call(functools.partial(kernel, n_rows, n_cols, x_his), out_shap...  106 us
    unnamed x4, local copies, waits for them, and re-layouts  5.54 us

profile of v4, /device:TPU:1, one launch (start us, length us, event | category | flops | bytes accessed | tf_op | source)
XLA Modules:
  0.0 114.1 jit_solution(14036739546374080890)
XLA Ops:
  0.6 0.9 select_reduce_fusion
  1.5 0.6 and_select_fusion.6
  2.1 0.2 convert_reduce_fusion
  2.3 0.1 select_reduce_fusion.1
  2.5 0.0 copy-start
  2.6 0.6 copy-done
  3.1 106.0 %shard_map.59 = (f32[2,128,512]{2,1,0:T(8,128)}, f32[2,512,512]{2,1,0:T(8,128)}) custom-call(bf16[26,128,1664]{2,1,0:T(8,128)(2,1)} %bitcast.50, bf16[2,512,512]{2,1,0:T(8,128)(2,1)} %pan.1, s32[2,64]{1,0:T(2,128)} %get-tuple-element.3.cols, s32[6,2,128]{2,1,0:T(2,128)} %copy-done), custom_call_target="tpu_custom_call" | custom-call | tf_op jit(solution)/shard_map/pallas_call | solution.py:572
  109.1 1.9 %copy.13 = f32[2,128,512]{2,1,0:T(8,128)} copy(f32[2,128,512]{2,1,0:T(8,128)} %get-tuple-element.7) | data formatting | bytes 1048576
  111.0 3.1 %copy.14 = f32[2,512,512]{2,1,0:T(8,128)} copy(f32[2,512,512]{2,1,0:T(8,128)} %get-tuple-element.8) | data formatting | bytes 4194304
  (8 shorter events, 0.1 us)
Async XLA Ops:
  2.5 0.6 copy-start

commit v5 on v4

--- a/solution.py
+++ b/solution.py
@@ -158,7 +158,6 @@
             remote(p_send.at[s, d], p_recv[s].at[core, source], p_ss.at[s, d], p_rs.at[s, d], sibling).wait_recv()
 
         b_copy(s, core).start()
-        b_copy(s, 1 - core).wait_recv()
 
     mine = pl.ds(core * chips, chips)
     x_lo, y = me_r // ys, lax.rem(me_r, ys)
@@ -193,6 +192,7 @@
         return remote(block, block, as_ss.at[s, source], as_rs.at[s, source], sibling)
 
     def pack(s):
+        b_copy(s, 1 - core).wait_recv()
         for t in range(chips):
             k = core * chips + t
             block = p_recv[s][by_k[5, s, chip * n_cols + k], by_k[1, s, chip * n_cols + k]]
@@ -272,8 +272,8 @@
     ag_first(0)
     picks(1)
     to_cores(1)
+    ag_second(0)
     pack(1)
-    ag_second(0)
     ag_first(1)
     l_first()
     ag_third(0)
@@ -291,25 +291,33 @@
         def _(source):
             as_copy(s, source, 1 - core).wait_recv()
 
-        @pl.loop(0, 2 * x_his)
-        def _(i):
-            half_of, h = i // x_his, lax.rem(i + 1 + x_hi, x_his)
+        def product(half_of, h):
             rows = pl.ds(pl.multiple_of((half_of * chips + h * zs) * BS, BS), zs * BS)
-            product = jnp.dot(a_pick[s, rows, :], p_all[s].reshape(n_cols * BS, width), preferred_element_type=F32)
-            part[s, half_of, h] = product.reshape(zs, BS, width)
-
-            @pl.when(half_of == 0)
-            def _():
-                c_copy(s, h).start()
-
-        for h in (1 - x_hi, x_hi):
+            result = jnp.dot(a_pick[s, rows, :], p_all[s].reshape(n_cols * BS, width), preferred_element_type=F32)
+            part[s, half_of, h] = result.reshape(zs, BS, width)
+
+        def to_z(h):
             c_copy(s, h).wait_recv()
 
             @pl.loop(1, zs)
-            def _(d, h=h):
+            def _(d):
                 there = lax.rem(z + d, zs)
                 encode(z_send.at[s, h, d - 1], part[s, 1, h, there] + core_recv[s, h, there])
                 z_copy(s, h, d).start()
+
+        @pl.loop(0, x_his)
+        def _(step):
+            h = jnp.where(step == 0, 1 - x_hi, x_hi)
+            product(0, h)
+            c_copy(s, h).start()
+
+            @pl.when(step > 0)
+            def _():
+                to_z(1 - x_hi)
+
+            product(1, h)
+
+        to_z(x_hi)
 
     products(0)
     l_second()
@@ -572,8 +580,8 @@
     return pl.pallas_call(
         functools.partial(kernel, n_rows, n_cols, x_his),
         out_shape=(
-            jax.ShapeDtypeStruct((supers, BS, width), F32),
-            jax.ShapeDtypeStruct((supers, width, width), F32),
+            pltpu.VMEM((supers, BS, width), F32),
+            pltpu.VMEM((supers, width, width), F32),
         ),
         in_specs=[pl.BlockSpec(memory_space=pl.ANY), vmem, smem, smem],
         out_specs=(vmem, vmem),

time: 114 us -> 108 us (0.947)
  Pallas kernels: 106 us -> 103 us
  local copies, waits for them, and re-layouts: 5.54 us -> 2.7 us
    pallas_call x1, Pallas kernels: 106 us -> 103 us  [local(): pl.pallas_call(functools.partial(kernel, n_rows, n_cols, x_his), out_shap...]
    unnamed x4, local copies, waits for them, and re-layouts: 5.54 us -> 2.7 us
where the time goes in v5:
time: 108 us
  Pallas kernels  103 us (95%)
  local copies, waits for them, and re-layouts  2.7 us (2%)
  other arithmetic  1.89 us (2%)
    pallas_call x1, Pallas kernels, local(): pl.pallas_call(functools.partial(kernel, n_rows, n_cols, x_his), out_shap...  103 us
    unnamed x4, local copies, waits for them, and re-layouts  2.7 us

profile of v5, /device:TPU:1, one launch (start us, length us, event | category | flops | bytes accessed | tf_op | source)
XLA Modules:
  0.0 108.3 jit_solution(14565836671693735434)
XLA Ops:
  0.6 0.9 select_reduce_fusion
  1.5 0.6 and_select_fusion.6
  2.1 0.2 convert_reduce_fusion
  2.3 0.1 select_reduce_fusion.1
  2.5 0.0 copy-start
  2.6 0.6 copy-done
  3.1 103.0 %shard_map.59 = (f32[2,128,512]{2,1,0:T(8,128)S(1)}, f32[2,512,512]{2,1,0:T(8,128)S(1)}) custom-call(bf16[26,128,1664]{2,1,0:T(8,128)(2,1)} %bitcast.50, bf16[2,512,512]{2,1,0:T(8,128)(2,1)} %pan.1, s32[2,64]{1,0:T(2,128)} %get-tuple-element.3.cols, s32[6,2,128]{2,1,0:T(2,128)} %copy-done), custom_call_target="tpu_custom_call" | custom-call | tf_op jit(solution)/shard_map/pallas_call | solution.py:580
  106.2 0.8 copy.13
  107.0 1.3 %copy.14 = f32[2,512,512]{2,1,0:T(8,128)} copy(f32[2,512,512]{2,1,0:T(8,128)S(1)} %get-tuple-element.6) | data formatting | bytes 4194304
  (8 shorter events, 0.1 us)
Async XLA Ops:
  2.5 0.6 copy-start

commit v6 on v5

--- a/solution.py
+++ b/solution.py
@@ -56,19 +56,19 @@
 
 def kernel(
     n_rows, n_cols, x_his,
-    inv_hbm, pan, cols, by_k,
+    inv_hbm, pan_hbm, cols, by_k,
     out, diag,
-    a_all, a_pick, p_send, p_recv_0, p_recv_1, p_all, l_recv, left,
+    pan, a_all, a_pick, p_send, p_recv_0, p_recv_1, p_all, l_recv, left,
     part, core_recv, z_send, z_recv, x_send, x_recv, d_part, d_sib, u_send, u_recv, v_send, v_recv, t_all,
-    a_sem, p_ss, p_rs, b_ss, b_rs, ag_ss, ag_rs, as_ss, as_rs, l_ss, l_rs, m_ss, m_rs, c_ss, c_rs, z_ss, z_rs, x_ss, x_rs,
+    pan_sem, a_sem, p_ss, p_rs, b_ss, b_rs, ag_ss, ag_rs, as_ss, as_rs, l_ss, l_rs, m_ss, m_rs, c_ss, c_rs, z_ss, z_rs, x_ss, x_rs,
     ds_ss, ds_rs, u_ss, u_rs, v_ss, v_rs, t_ss, t_rs, w_ss, w_rs, er_ss, er_rs, es_ss, es_rs,
 ):
     supers = pan.shape[0]
     p_recv = (p_recv_0, p_recv_1)
     sub = BS // n_rows
     col_blocks = a_all.shape[0]
-    shard = pan.shape[1] // BS
-    width = pan.shape[2]
+    shard = pan.shape[1]
+    width = pan.shape[3]
     chips = n_cols // 2
     zs = chips // x_his
     ys = n_rows // 2
@@ -83,6 +83,22 @@
             src_ref=src, dst_ref=dst, send_sem=ss, recv_sem=rs, device_id=to, device_id_type=MESH
         )
 
+    barrier = pltpu.get_barrier_semaphore()
+
+    @pl.loop(1, n_cols)
+    def _(d):
+        pl.semaphore_signal(barrier, inc=1, device_id=(me_r, lax.rem(me_c + d, n_cols)), device_id_type=MESH)
+
+    @pl.loop(1, n_rows)
+    def _(d):
+        pl.semaphore_signal(barrier, inc=1, device_id=(lax.rem(me_r + d, n_rows), me_c), device_id_type=MESH)
+
+    opposite = (lax.rem(me_r + ys, n_rows), lax.rem(me_c + zs * 2, n_cols))
+    pl.semaphore_signal(barrier, inc=1, device_id=opposite, device_id_type=MESH)
+
+    load_pan = pltpu.make_async_copy(pan_hbm.at[:, :, me_r], pan, pan_sem)
+    load_pan.start()
+
     def load_a(b):
         columns = pl.ds(pl.multiple_of(b * BS, BS), BS)
         return pltpu.make_async_copy(inv_hbm.at[:, :, columns], a_all.at[b], a_sem.at[b])
@@ -91,24 +107,12 @@
     def _(b):
         load_a(b).start()
 
-    barrier = pltpu.get_barrier_semaphore()
-
-    @pl.loop(1, n_cols)
-    def _(d):
-        pl.semaphore_signal(barrier, inc=1, device_id=(me_r, lax.rem(me_c + d, n_cols)), device_id_type=MESH)
-
-    @pl.loop(1, n_rows)
-    def _(d):
-        pl.semaphore_signal(barrier, inc=1, device_id=(lax.rem(me_r + d, n_rows), me_c), device_id_type=MESH)
-
-    opposite = (lax.rem(me_r + ys, n_rows), lax.rem(me_c + zs * 2, n_cols))
-    pl.semaphore_signal(barrier, inc=1, device_id=opposite, device_id_type=MESH)
+    load_pan.wait()
 
     def pick_for(c, s):
         piece = jnp.zeros((sub, width), BF16)
         for q in range(shard):
-            block = pan[s, pl.ds(pl.multiple_of(q * BS + me_r * sub, sub), sub), :]
-            piece = jnp.where(cols[s, me_c * shard + q] == c, block, piece)
+            piece = jnp.where(cols[s, me_c * shard + q] == c, pan[s, q], piece)
         return piece
 
     @pl.loop(1, n_cols)
@@ -320,8 +324,8 @@
         to_z(x_hi)
 
     products(0)
+    ag_third(1)
     l_second()
-    ag_third(1)
     products(1)
 
     @pl.loop(1, n_rows)
@@ -534,10 +538,12 @@
     half = width // 2
     lists = tables(block_slot, list_ids, n_rows, n_cols)
     blocks = inverse.reshape(-1, BS, inverse.shape[1])
+    slices = panels.reshape(supers, -1, n_rows, sub, width)
     vmem = pl.BlockSpec(memory_space=pltpu.VMEM)
     smem = pl.BlockSpec(memory_space=pltpu.SMEM)
     dma = pltpu.SemaphoreType.DMA
     scratch = [
+        pltpu.VMEM((supers, slices.shape[1], sub, width), BF16),
         pltpu.VMEM((col_blocks, blocks.shape[0], BS, BS), BF16),
         pltpu.VMEM((supers, n_cols * BS, n_cols * BS), BF16),
         pltpu.VMEM((supers, n_cols, sub, width), BF16),
@@ -559,6 +565,7 @@
         pltpu.VMEM((supers, 2, zs, half // zs // zs, half), F32),
         pltpu.VMEM((supers, 2, zs, half // zs // zs, half), F32),
         pltpu.VMEM((supers, 2, zs, half // zs // zs, half), F32),
+        dma(()),
         dma((col_blocks,)),
         dma((supers, n_cols)), dma((supers, n_cols)),
         dma((supers,)), dma((supers,)),
@@ -583,13 +590,13 @@
             pltpu.VMEM((supers, BS, width), F32),
             pltpu.VMEM((supers, width, width), F32),
         ),
-        in_specs=[pl.BlockSpec(memory_space=pl.ANY), vmem, smem, smem],
+        in_specs=[pl.BlockSpec(memory_space=pl.ANY), pl.BlockSpec(memory_space=pl.ANY), smem, smem],
         out_specs=(vmem, vmem),
         scratch_shapes=scratch,
         compiler_params=pltpu.CompilerParams(
             collective_id=0, has_side_effects=True, vmem_limit_bytes=60 * 2**20
         ),
-    )(blocks, panels, *lists)
+    )(blocks, slices, *lists)
 
 
 def solution(mesh):

time: 108 us -> 106 us (0.981)
  Pallas kernels: 103 us -> 101 us
    pallas_call x1, Pallas kernels: 103 us -> 101 us  [local(): pl.pallas_call(functools.partial(kernel, n_rows, n_cols, x_his), out_shap...]
where the time goes in v6:
time: 106 us
  Pallas kernels  101 us (95%)
  local copies, waits for them, and re-layouts  2.7 us (3%)
  other arithmetic  1.89 us (2%)
    pallas_call x1, Pallas kernels, local(): pl.pallas_call(functools.partial(kernel, n_rows, n_cols, x_his), out_shap...  101 us
    unnamed x4, local copies, waits for them, and re-layouts  2.7 us

profile of v6, /device:TPU:1, one launch (start us, length us, event | category | flops | bytes accessed | tf_op | source)
XLA Modules:
  0.0 106.0 jit_solution(2780470355300571866)
XLA Ops:
  0.6 0.9 select_reduce_fusion
  1.5 0.6 and_select_fusion.6
  2.1 0.2 convert_reduce_fusion
  2.3 0.1 select_reduce_fusion.1
  2.5 0.0 copy-start
  2.6 0.6 copy-done
  3.1 100.7 %shard_map.59 = (f32[2,128,512]{2,1,0:T(8,128)S(1)}, f32[2,512,512]{2,1,0:T(8,128)S(1)}) custom-call(bf16[26,128,1664]{2,1,0:T(8,128)(2,1)} %bitcast.51, bf16[2,4,8,16,512]{4,3,2,1,0:T(8,128)(2,1)} %bitcast.52, s32[2,64]{1,0:T(2,128)} %get-tuple-element.3.cols, s32[6,2,128]{2,1,0:T(2,128)} %copy-done), custom_call_target="tpu_custom_call" | custom-call | tf_op jit(solution)/shard_map/pallas_call | solution.py:587
  103.9 0.8 copy.13
  104.7 1.3 %copy.14 = f32[2,512,512]{2,1,0:T(8,128)} copy(f32[2,512,512]{2,1,0:T(8,128)S(1)} %get-tuple-element.6) | data formatting | bytes 4194304
  (8 shorter events, 0.1 us)
Async XLA Ops:
  2.5 0.6 copy-start

commit v7 on v6

--- a/solution.py
+++ b/solution.py
@@ -169,27 +169,24 @@
     far = x_lo * ys + lax.rem(y + 2, ys)
     far_up, far_down = lax.rem(up + ys, n_rows), lax.rem(down + ys, n_rows)
     far_far = lax.rem(far + ys, n_rows)
-    first = pl.ds(core * chips, chips // 2)
-    second = pl.ds(core * chips + chips // 2, chips // 2)
-
-    def ag_copy(s, j, slots, source, to):
-        block = p_all.at[s, slots, source]
+
+    def ag_copy(s, j, source, to):
+        block = p_all.at[s, mine, source]
         return remote(block, block, ag_ss.at[s, j], ag_rs.at[s, j], (to, me_c))
 
     sends = {
-        0: (mine, me_r, up), 1: (mine, me_r, down), 2: (mine, me_r, across),
-        3: (first, down, up), 4: (second, up, down), 5: (mine, across, up), 6: (mine, across, down), 7: (mine, far, across),
+        0: (me_r, up), 1: (me_r, down), 2: (me_r, across), 3: (me_r, far),
+        4: (across, up), 5: (across, down), 6: (far, across),
     }
     arrivals = {
-        0: (mine, down), 1: (mine, up), 2: (mine, across),
-        3: (first, far), 4: (second, far), 5: (mine, far_down), 6: (mine, far_up), 7: (mine, far_far),
+        0: down, 1: up, 2: across, 3: far, 4: far_down, 5: far_up, 6: far_far,
     }
 
     def ag_start(s, j):
         ag_copy(s, j, *sends[j]).start()
 
     def ag_wait(s, j):
-        ag_copy(s, j, *arrivals[j], across).wait_recv()
+        ag_copy(s, j, arrivals[j], across).wait_recv()
 
     def as_copy(s, source, of):
         block = p_all.at[s, pl.ds(of * chips, chips), source]
@@ -204,31 +201,26 @@
             p_all[s, k, me_r] = jnp.where(valid, block, jnp.zeros_like(block))
 
     def ag_first(s):
-        for j in (0, 1, 2):
+        for j in (2, 0, 1, 3):
             ag_start(s, j)
         as_copy(s, me_r, core).start()
 
     def ag_second(s):
         ag_wait(s, 2)
+        ag_start(s, 4)
         ag_start(s, 5)
-        ag_start(s, 6)
         ag_wait(s, 0)
-        ag_start(s, 3)
         ag_wait(s, 1)
-        ag_start(s, 4)
         for source in (across, down, up):
             as_copy(s, source, core).start()
 
     def ag_third(s):
         ag_wait(s, 3)
-        ag_wait(s, 4)
-        ag_start(s, 7)
-        ag_wait(s, 5)
-        ag_wait(s, 6)
-        for source in (far, far_down, far_up):
+        ag_start(s, 6)
+        as_copy(s, far, core).start()
+        for j, source in ((4, far_down), (5, far_up), (6, far_far)):
+            ag_wait(s, j)
             as_copy(s, source, core).start()
-        ag_wait(s, 7)
-        as_copy(s, far_far, core).start()
 
     def l_copy(t):
         k = core * chips + t

time: 106 us -> 106 us (level)
  no operation moved by 1% of the time
where the time goes in v7:
time: 106 us
  Pallas kernels  101 us (95%)
  local copies, waits for them, and re-layouts  2.7 us (3%)
  other arithmetic  1.89 us (2%)
    pallas_call x1, Pallas kernels, local(): pl.pallas_call(functools.partial(kernel, n_rows, n_cols, x_his), out_shap...  101 us
    unnamed x4, local copies, waits for them, and re-layouts  2.7 us

profile of v7, /device:TPU:1, one launch (start us, length us, event | category | flops | bytes accessed | tf_op | source)
XLA Modules:
  0.0 106.0 jit_solution(9257779997354426135)
XLA Ops:
  0.6 0.9 select_reduce_fusion
  1.5 0.6 and_select_fusion.6
  2.1 0.2 convert_reduce_fusion
  2.3 0.1 select_reduce_fusion.1
  2.5 0.0 copy-start
  2.6 0.6 copy-done
  3.1 100.8 %shard_map.59 = (f32[2,128,512]{2,1,0:T(8,128)S(1)}, f32[2,512,512]{2,1,0:T(8,128)S(1)}) custom-call(bf16[26,128,1664]{2,1,0:T(8,128)(2,1)} %bitcast.51, bf16[2,4,8,16,512]{4,3,2,1,0:T(8,128)(2,1)} %bitcast.52, s32[2,64]{1,0:T(2,128)} %get-tuple-element.3.cols, s32[6,2,128]{2,1,0:T(2,128)} %copy-done), custom_call_target="tpu_custom_call" | custom-call | tf_op jit(solution)/shard_map/pallas_call | solution.py:579
  103.9 0.8 copy.13
  104.7 1.3 %copy.14 = f32[2,512,512]{2,1,0:T(8,128)} copy(f32[2,512,512]{2,1,0:T(8,128)S(1)} %get-tuple-element.6) | data formatting | bytes 4194304
  (8 shorter events, 0.1 us)
Async XLA Ops:
  2.5 0.6 copy-start

commit v8 on v6

--- a/solution.py
+++ b/solution.py
@@ -43,7 +43,7 @@
 def encode(ref, block):
     top = jnp.max(jnp.abs(block), axis=0, keepdims=True)
     exponent = jnp.floor(jnp.log2(jnp.maximum(top, 1e-30))) + 1.0
-    coded = jnp.round(block * (jnp.exp2(-exponent) * TOP))
+    coded = jnp.floor(block * (jnp.exp2(-exponent) * TOP) + 0.5)
     ref[0:BS] = coded.astype(jnp.int32).astype(jnp.int16)
     exponents = jnp.broadcast_to(exponent, (SCALE_ROWS, block.shape[1]))
     ref[BS : BS + SCALE_ROWS] = exponents.astype(jnp.int32).astype(jnp.int16)
@@ -469,8 +469,8 @@
 
     start_x(0)
     finish_sums(0)
+    start_x(1)
     over_cores(0)
-    start_x(1)
     over_first(0)
     finish_sums(1)
     over_second(0)

time: 106 us -> 106 us (level)
  no operation moved by 1% of the time
where the time goes in v8:
time: 106 us
  Pallas kernels  101 us (95%)
  local copies, waits for them, and re-layouts  2.7 us (3%)
  other arithmetic  1.89 us (2%)
    pallas_call x1, Pallas kernels, local(): pl.pallas_call(functools.partial(kernel, n_rows, n_cols, x_his), out_shap...  101 us
    unnamed x4, local copies, waits for them, and re-layouts  2.7 us

profile of v8, /device:TPU:1, one launch (start us, length us, event | category | flops | bytes accessed | tf_op | source)
XLA Modules:
  0.0 106.0 jit_solution(12868652736919214665)
XLA Ops:
  0.6 0.9 select_reduce_fusion
  1.5 0.6 and_select_fusion.6
  2.1 0.2 convert_reduce_fusion
  2.3 0.1 select_reduce_fusion.1
  2.5 0.0 copy-start
  2.6 0.6 copy-done
  3.1 100.7 %shard_map.59 = (f32[2,128,512]{2,1,0:T(8,128)S(1)}, f32[2,512,512]{2,1,0:T(8,128)S(1)}) custom-call(bf16[26,128,1664]{2,1,0:T(8,128)(2,1)} %bitcast.51, bf16[2,4,8,16,512]{4,3,2,1,0:T(8,128)(2,1)} %bitcast.52, s32[2,64]{1,0:T(2,128)} %get-tuple-element.3.cols, s32[6,2,128]{2,1,0:T(2,128)} %copy-done), custom_call_target="tpu_custom_call" | custom-call | tf_op jit(solution)/shard_map/pallas_call | solution.py:587
  103.9 0.8 copy.13
  104.7 1.3 %copy.14 = f32[2,512,512]{2,1,0:T(8,128)} copy(f32[2,512,512]{2,1,0:T(8,128)S(1)} %get-tuple-element.6) | data formatting | bytes 4194304
  (8 shorter events, 0.1 us)
Async XLA Ops:
  2.5 0.6 copy-start
